TPU v7x, 512 devices: a whole 4x4x16 slice. The times are simulated.
512 devices in a mesh: vec: 16 (over x, z_hi, core), lat: 32 (over z_lo, y).
Axes of the slice: x: 4, y: 4, z: 16 (z_hi: 2, z_lo: 8; z = z_hi * 8 + z_lo), core: 2. Of those that a mesh axis runs over, the one named last changes fastest.
Arguments:
- perturbation: float32 [128, 3, 256, 2048], P('vec', None, 'lat'), may hold values from -6 to 6
- wind_coriolis: float32 [4, 3, 256, 2048], P(None, None, 'lat', 'vec'), may hold values from -4 to 4
- depth_field: float32 [4, 256, 2048], P(None, 'lat', 'vec'), may hold values from 0.5 to 2
Outputs:
- evolved: float32 [128, 3, 256, 2048], P('vec', None, 'lat')
All inputs are finite; a program needn't handle non-finite values.
Results may differ from a plain program's by a relative error of at most 0.00002.
Values sent between devices are 32-bit elements; how exact they have to be, the bound alone decides.
No kernel may reach another device: no remote copies, remote signals or barrier semaphores. Data moves between devices by JAX's collectives and lax.ppermute only.
A program may use at most 64 MiB of HBM per device.

v0:
```python
import jax
import jax.numpy as jnp
from jax import lax
from jax.sharding import PartitionSpec as P

STEPS = 4


time_step = 0.2
viscosity = 0.05


def laid_out(tiles, dim):
    lengths = list(tiles.shape[1:])
    lengths[dim] *= tiles.shape[0]
    return jnp.moveaxis(tiles, 0, dim).reshape(lengths)


def sent_to_all(shard, axis):
    count = lax.axis_size(axis)
    return lax.all_to_all(
        jnp.broadcast_to(shard[None], (count, *shard.shape)), axis, 0, 0, tiled=True
    )


def gathered_copies(shard, axis, dim):
    return laid_out(sent_to_all(shard, axis), dim)


def extended(shard, sides, width):
    for axis, dim in sides:
        count, length = (lax.axis_size(axis), shard.shape[dim])
        up = [(i, (i + 1) % count) for i in range(count - 1)]
        down = [(j, i) for i, j in up]
        last = lax.slice_in_dim(shard, length - width, length, axis=dim)
        leading = lax.slice_in_dim(shard, 0, width, axis=dim)
        before = lax.ppermute(last, axis, up)
        after = lax.ppermute(leading, axis, down)
        shard = jnp.concatenate([before, shard, after], axis=dim)
    return shard


def lon_diff(field):
    return 0.5 * (jnp.roll(field, -1, axis=-1) - jnp.roll(field, 1, axis=-1))


def lat_diff(padded):
    return 0.5 * (padded[..., 2:, :] - padded[..., :-2, :])


def smooth(padded, centre):
    return (
        padded[..., 2:, :]
        + padded[..., :-2, :]
        + jnp.roll(centre, -1, axis=-1)
        + jnp.roll(centre, 1, axis=-1)
        - 4.0 * centre
    )


def advance(padded, coefficients):
    height_pad = padded[..., 0, :, :]
    zonal_pad = padded[..., 1, :, :]
    north_pad = padded[..., 2, :, :]
    height = height_pad[..., 1:-1, :]
    zonal = zonal_pad[..., 1:-1, :]
    north = north_pad[..., 1:-1, :]
    east_wind = coefficients[0]
    north_wind = coefficients[1]
    rotation = coefficients[2]
    depth_now = coefficients[3]
    tend_height = -(
        east_wind * lon_diff(height)
        + north_wind * lat_diff(height_pad)
        + depth_now * (lon_diff(zonal) + lat_diff(north_pad))
    )
    tend_zonal = (
        -(east_wind * lon_diff(zonal) + north_wind * lat_diff(zonal_pad))
        + rotation * north
        - lon_diff(height)
    )
    tend_north = (
        -(east_wind * lon_diff(north) + north_wind * lat_diff(north_pad))
        - rotation * zonal
        - lat_diff(height_pad)
    )
    new_height = height + time_step * (tend_height + viscosity * smooth(height_pad, height))
    new_zonal = zonal + time_step * (tend_zonal + viscosity * smooth(zonal_pad, zonal))
    new_north = north + time_step * (tend_north + viscosity * smooth(north_pad, north))
    return jnp.stack([new_height, new_zonal, new_north], axis=-3)


def shards(perturbation, wind_coriolis, depth_field):
    coefficients = jnp.concatenate([wind_coriolis, depth_field[:, None]], axis=1)
    state = perturbation
    for moment in range(STEPS):
        gathered = gathered_copies(coefficients[moment], "vec", 2)
        padded = extended(state, (("lat", 2),), 1)
        state = advance(padded, gathered)
    return state


def solution(mesh):
    placed = (P("vec", None, "lat", None), P(None, None, "lat", "vec"), P(None, "lat", "vec"))
    return jax.shard_map(
        shards, mesh=mesh, in_specs=placed, out_specs=P("vec", None, "lat", None), check_vma=False
    )
```

profile of v0, /device:TPU:33, one launch (start us, length us, event | category | flops | bytes accessed | tf_op | source)
XLA Modules:
  0.0 143.7 jit_solution(9258925399185701110)
XLA Ops:
  0.0 2.2 %fusion.27 = (f32[8,3,1,2048]{3,2,0,1:T(1,128)S(1)}, f32[8,3,1,2048]{3,2,0,1:T(1,128)S(1)}) fusion(f32[8,3,8,2048]{3,2,1,0:T(8,128)} %param.3), kind=kLoop, calls=%fused_computation.120 | loop fusion | bytes 786432 | tf_op jit(solution)/shard_map/slice | solution.py:35
  2.3 3.2 %collective-permute-start = (f32[8,3,1,2048]{3,2,0,1:T(1,128)S(1)}, f32[8,3,1,2048]{3,2,0,1:T(1,128)S(1)}, u32[]{:S(2)}, u32[]{:S(2)}) collective-permute-start(f32[8,3,1,2048]{3,2,0,1:T(1,128)S(1)} %get-tuple-element.23), channel_id=1, source_target_pairs={{0,1},{1,2},{2,3},{3,4},{4,5},{5,6},{6,7},{7,8},{8,9},{9,10},{10,1... | collective-permute-start | bytes 589832 | tf_op jit(solution)/shard_map/ppermute | solution.py:37
  5.5 4.2 %collective-permute-start.1 = (f32[8,3,1,2048]{3,2,0,1:T(1,128)S(1)}, f32[8,3,1,2048]{3,2,0,1:T(1,128)S(1)}, u32[]{:S(2)}, u32[]{:S(2)}) collective-permute-start(f32[8,3,1,2048]{3,2,0,1:T(1,128)S(1)} %get-tuple-element.24), channel_id=1, source_target_pairs={{1,0},{2,1},{3,2},{4,3},{5,4},{6,5},{7,6},{8,7},{9,8},{10,9},{11,1... | collective-permute-start | bytes 589832 | tf_op jit(solution)/shard_map/ppermute | solution.py:38
  9.7 1.4 fusion.26
  11.1 0.7 broadcast_in_dim.33
  11.8 17.9 %all-to-all-start = ((f32[16,4,8,128]{3,2,1,0:T(8,128)}), f32[16,4,8,128]{3,2,1,0:T(8,128)S(1)}, u32[]{:S(2)}, u32[]{:S(2)}) async-start(f32[16,4,8,128]{3,2,1,0:T(8,128)} %broadcast_in_dim.33), calls=%async_computation | async-start | bytes 524288 | tf_op jit(solution)/shard_map/all_to_all | solution.py:21
  29.7 1.9 %pad_maximum_fusion = f32[8,3,10,2048]{3,2,0,1:T(8,128)S(1)} fusion(f32[8,3,1,2048]{3,2,0,1:T(1,128)S(1)} %collective-permute-done.1, f32[8,3,1,2048]{3,2,0,1:T(1,128)S(1)} %collective-permute-done, f32[8,3,8,2048]{3,2,1,0:T(8,128)} %param.3), kind=kLoop, calls=%fused_computation | loop fusion | flops 983040 | bytes 3932160 | tf_op jit(solution)/shard_map/concatenate | solution.py:39
  31.9 0.7 fusion.51
  32.7 1.2 fusion.50
  33.8 1.6 %fusion.46 = (f32[8,8,2047]{2,1,0:T(8,128)}, f32[8,8,2047]{2,1,0:T(8,128)}, f32[8,8,2047]{2,1,0:T(8,128)}, f32[8,8,2047]{2,1,0:T(8,128)}) fusion(f32[8,10,2048]{2,1,0:T(8,128)S(1)} %get-tuple-element.14, f32[8,10,2048]{2,1,0:T(8,128)S(1)} %get-tuple-element.16), kind=kLoop, calls=%fused_computation.139 | loop fusion | bytes 4192256 | tf_op jit(solution)/shard_map/jit(_roll_static)/slice | solution.py:44
  35.5 18.6 %all-to-all-done = f32[16,4,8,128]{3,2,1,0:T(8,128)S(1)} async-done(((f32[16,4,8,128]{3,2,1,0:T(8,128)}), f32[16,4,8,128]{3,2,1,0:T(8,128)S(1)}, u32[]{:S(2)}, u32[]{:S(2)}) %all-to-all-start) | async-done | bytes 262176 | tf_op jit(solution)/shard_map/all_to_all | solution.py:21
  54.0 1.4 broadcast_in_dim.35
  55.5 4.3 %all-to-all-start.1 = ((f32[16,4,8,128]{3,2,1,0:T(8,128)}), f32[16,4,8,128]{3,2,1,0:T(8,128)S(1)}, u32[]{:S(2)}, u32[]{:S(2)}) async-start(f32[16,4,8,128]{3,2,1,0:T(8,128)} %broadcast_in_dim.35), calls=%async_computation.1 | async-start | bytes 524288 | tf_op jit(solution)/shard_map/all_to_all | solution.py:21
  59.8 1.1 fusion.17
  60.9 2.1 %add_bitcast_fusion.11 = f32[8,1,8,2048]{3,2,0,1:T(8,128)S(1)} fusion(f32[8,10,2048]{2,1,0:T(8,128)S(1)} %get-tuple-element.14, f32[8,8,2047]{2,1,0:T(8,128)} %get-tuple-element.93, f32[8,8,1]{2,1,0:T(8,128)S(1)} %get-tuple-element.95, f32[8,8,1]{2,1,0:T(8,128)S(1)} %get-tuple-element.96, f32[8,8,2047]{2,1,0:T(8,128)} %get-tuple-element.94, ...), kind=kLoop, calls=%fused_computation.52 | loop fusion | flops 3145728 | bytes 5439488 | tf_op jit(solution)/shard_map/stack | solution.py:90
  63.1 0.6 add_bitcast_fusion.10
  65.8 1.9 %collective-permute-start.2 = (f32[8,3,1,2048]{3,2,0,1:T(1,128)S(1)}, f32[8,3,1,2048]{3,2,0,1:T(1,128)S(1)}, u32[]{:S(2)}, u32[]{:S(2)}) collective-permute-start(f32[8,3,1,2048]{3,2,0,1:T(1,128)S(1)} %get-tuple-element.21), channel_id=1, source_target_pairs={{0,1},{1,2},{2,3},{3,4},{4,5},{5,6},{6,7},{7,8},{8,9},{9,10},{10,1... | collective-permute-start | bytes 589832 | tf_op jit(solution)/shard_map/ppermute | solution.py:37
  67.7 5.5 %collective-permute-start.3 = (f32[8,3,1,2048]{3,2,0,1:T(1,128)S(1)}, f32[8,3,1,2048]{3,2,0,1:T(1,128)S(1)}, u32[]{:S(2)}, u32[]{:S(2)}) collective-permute-start(f32[8,3,1,2048]{3,2,0,1:T(1,128)S(1)} %get-tuple-element.22), channel_id=1, source_target_pairs={{1,0},{2,1},{3,2},{4,3},{5,4},{6,5},{7,6},{8,7},{9,8},{10,9},{11,1... | collective-permute-start | bytes 589832 | tf_op jit(solution)/shard_map/ppermute | solution.py:38
  73.2 6.3 %all-to-all-done.1 = f32[16,4,8,128]{3,2,1,0:T(8,128)S(1)} async-done(((f32[16,4,8,128]{3,2,1,0:T(8,128)}), f32[16,4,8,128]{3,2,1,0:T(8,128)S(1)}, u32[]{:S(2)}, u32[]{:S(2)}) %all-to-all-start.1) | async-done | bytes 262176 | tf_op jit(solution)/shard_map/all_to_all | solution.py:21
  79.5 0.7 broadcast_in_dim.37
  80.2 8.8 %all-to-all-start.2 = ((f32[16,4,8,128]{3,2,1,0:T(8,128)}), f32[16,4,8,128]{3,2,1,0:T(8,128)S(1)}, u32[]{:S(2)}, u32[]{:S(2)}) async-start(f32[16,4,8,128]{3,2,1,0:T(8,128)} %broadcast_in_dim.37), calls=%async_computation.2 | async-start | bytes 524288 | tf_op jit(solution)/shard_map/all_to_all | solution.py:21
  89.1 1.9 %pad_maximum_fusion.1 = f32[8,3,10,2048]{3,2,0,1:T(8,128)S(1)} fusion(f32[8,3,1,2048]{3,2,0,1:T(1,128)S(1)} %collective-permute-done.3, f32[8,1,8,2048]{3,2,0,1:T(8,128)} %copy-done.1, f32[8,1,8,2048]{3,2,0,1:T(8,128)} %copy-done, f32[8,1,8,2048]{3,2,0,1:T(8,128)} %copy-done.2, f32[8,3,1,2048]{3,2,0,1:T(1,128)S(1)} %collective-permute-done.2), kind=kLoop, calls=%fused_computation.1 | loop fusion | flops 1966080 | bytes 3932160 | tf_op jit(solution)/shard_map/concatenate | solution.py:39
  92.5 0.6 add_bitcast_fusion.7
  94.3 1.9 %collective-permute-start.4 = (f32[8,3,1,2048]{3,2,0,1:T(1,128)S(1)}, f32[8,3,1,2048]{3,2,0,1:T(1,128)S(1)}, u32[]{:S(2)}, u32[]{:S(2)}) collective-permute-start(f32[8,3,1,2048]{3,2,0,1:T(1,128)S(1)} %get-tuple-element.19), channel_id=1, source_target_pairs={{0,1},{1,2},{2,3},{3,4},{4,5},{5,6},{6,7},{7,8},{8,9},{9,10},{10,1... | collective-permute-start | bytes 589832 | tf_op jit(solution)/shard_map/ppermute | solution.py:37
  96.2 5.5 %collective-permute-start.5 = (f32[8,3,1,2048]{3,2,0,1:T(1,128)S(1)}, f32[8,3,1,2048]{3,2,0,1:T(1,128)S(1)}, u32[]{:S(2)}, u32[]{:S(2)}) collective-permute-start(f32[8,3,1,2048]{3,2,0,1:T(1,128)S(1)} %get-tuple-element.20), channel_id=1, source_target_pairs={{1,0},{2,1},{3,2},{4,3},{5,4},{6,5},{7,6},{8,7},{9,8},{10,9},{11,1... | collective-permute-start | bytes 589832 | tf_op jit(solution)/shard_map/ppermute | solution.py:38
  101.7 8.6 %all-to-all-done.2 = f32[16,4,8,128]{3,2,1,0:T(8,128)S(1)} async-done(((f32[16,4,8,128]{3,2,1,0:T(8,128)}), f32[16,4,8,128]{3,2,1,0:T(8,128)S(1)}, u32[]{:S(2)}, u32[]{:S(2)}) %all-to-all-start.2) | async-done | bytes 262176 | tf_op jit(solution)/shard_map/all_to_all | solution.py:21
  110.4 0.7 broadcast_in_dim.39
  111.1 6.3 %all-to-all-start.3 = ((f32[16,4,8,128]{3,2,1,0:T(8,128)}), f32[16,4,8,128]{3,2,1,0:T(8,128)S(1)}, u32[]{:S(2)}, u32[]{:S(2)}) async-start(f32[16,4,8,128]{3,2,1,0:T(8,128)} %broadcast_in_dim.39), calls=%async_computation.3 | async-start | bytes 524288 | tf_op jit(solution)/shard_map/all_to_all | solution.py:21
  121.4 1.9 %collective-permute-start.6 = (f32[8,3,1,2048]{3,2,0,1:T(1,128)S(1)}, f32[8,3,1,2048]{3,2,0,1:T(1,128)S(1)}, u32[]{:S(2)}, u32[]{:S(2)}) collective-permute-start(f32[8,3,1,2048]{3,2,0,1:T(1,128)S(1)} %get-tuple-element.17), channel_id=1, source_target_pairs={{0,1},{1,2},{2,3},{3,4},{4,5},{5,6},{6,7},{7,8},{8,9},{9,10},{10,1... | collective-permute-start | bytes 589832 | tf_op jit(solution)/shard_map/ppermute | solution.py:37
  123.3 5.5 %collective-permute-start.7 = (f32[8,3,1,2048]{3,2,0,1:T(1,128)S(1)}, f32[8,3,1,2048]{3,2,0,1:T(1,128)S(1)}, u32[]{:S(2)}, u32[]{:S(2)}) collective-permute-start(f32[8,3,1,2048]{3,2,0,1:T(1,128)S(1)} %get-tuple-element.18), channel_id=1, source_target_pairs={{1,0},{2,1},{3,2},{4,3},{5,4},{6,5},{7,6},{8,7},{9,8},{10,9},{11,1... | collective-permute-start | bytes 589832 | tf_op jit(solution)/shard_map/ppermute | solution.py:38
  128.8 10.0 %all-to-all-done.3 = f32[16,4,8,128]{3,2,1,0:T(8,128)S(1)} async-done(((f32[16,4,8,128]{3,2,1,0:T(8,128)}), f32[16,4,8,128]{3,2,1,0:T(8,128)S(1)}, u32[]{:S(2)}, u32[]{:S(2)}) %all-to-all-start.3) | async-done | bytes 262176 | tf_op jit(solution)/shard_map/all_to_all | solution.py:21
  142.4 1.3 pad_maximum_fusion.4
  (74 shorter events, 12.5 us)
Async XLA Ops:
  2.3 27.5 %collective-permute-start = (f32[8,3,1,2048]{3,2,0,1:T(1,128)S(1)}, f32[8,3,1,2048]{3,2,0,1:T(1,128)S(1)}, u32[]{:S(2)}, u32[]{:S(2)}) collective-permute-start(f32[8,3,1,2048]{3,2,0,1:T(1,128)S(1)} %get-tuple-element.23), channel_id=1, source_target_pairs={{0,1},{1,2},{2,3},{3,4},{4,5},{5,6},{6,7},{7,8},{8,9},{9,10},{10,1... | collective-permute-start | bytes 589832 | tf_op jit(solution)/shard_map/ppermute | solution.py:37
  5.5 24.3 %collective-permute-start.1 = (f32[8,3,1,2048]{3,2,0,1:T(1,128)S(1)}, f32[8,3,1,2048]{3,2,0,1:T(1,128)S(1)}, u32[]{:S(2)}, u32[]{:S(2)}) collective-permute-start(f32[8,3,1,2048]{3,2,0,1:T(1,128)S(1)} %get-tuple-element.24), channel_id=1, source_target_pairs={{1,0},{2,1},{3,2},{4,3},{5,4},{6,5},{7,6},{8,7},{9,8},{10,9},{11,1... | collective-permute-start | bytes 589832 | tf_op jit(solution)/shard_map/ppermute | solution.py:38
  11.8 42.2 %all-to-all-start = ((f32[16,4,8,128]{3,2,1,0:T(8,128)}), f32[16,4,8,128]{3,2,1,0:T(8,128)S(1)}, u32[]{:S(2)}, u32[]{:S(2)}) async-start(f32[16,4,8,128]{3,2,1,0:T(8,128)} %broadcast_in_dim.33), calls=%async_computation | async-start | bytes 524288 | tf_op jit(solution)/shard_map/all_to_all | solution.py:21
  54.0 1.4 copy-start.9
  55.5 24.0 %all-to-all-start.1 = ((f32[16,4,8,128]{3,2,1,0:T(8,128)}), f32[16,4,8,128]{3,2,1,0:T(8,128)S(1)}, u32[]{:S(2)}, u32[]{:S(2)}) async-start(f32[16,4,8,128]{3,2,1,0:T(8,128)} %broadcast_in_dim.35), calls=%async_computation.1 | async-start | bytes 524288 | tf_op jit(solution)/shard_map/all_to_all | solution.py:21
  59.8 3.3 %copy-start.3 = (f32[8,8,2047]{2,1,0:T(8,128)S(1)}, f32[8,8,2047]{2,1,0:T(8,128)}, u32[]{:S(2)}) copy-start(f32[8,8,2047]{2,1,0:T(8,128)} %get-tuple-element.61) | copy-start | bytes 1572100
  59.8 3.3 %copy-start.4 = (f32[8,8,2047]{2,1,0:T(8,128)S(1)}, f32[8,8,2047]{2,1,0:T(8,128)}, u32[]{:S(2)}) copy-start(f32[8,8,2047]{2,1,0:T(8,128)} %get-tuple-element.62) | copy-start | bytes 1572100
  59.8 3.3 %copy-start.5 = (f32[8,8,2047]{2,1,0:T(8,128)S(1)}, f32[8,8,2047]{2,1,0:T(8,128)}, u32[]{:S(2)}) copy-start(f32[8,8,2047]{2,1,0:T(8,128)} %get-tuple-element.93) | copy-start | bytes 1572100
  59.8 3.3 %copy-start.6 = (f32[8,8,2047]{2,1,0:T(8,128)S(1)}, f32[8,8,2047]{2,1,0:T(8,128)}, u32[]{:S(2)}) copy-start(f32[8,8,2047]{2,1,0:T(8,128)} %get-tuple-element.94) | copy-start | bytes 1572100
  63.0 2.0 %copy-start.2 = (f32[8,1,8,2048]{3,2,0,1:T(8,128)}, f32[8,1,8,2048]{3,2,0,1:T(8,128)S(1)}, u32[]{:S(2)}) copy-start(f32[8,1,8,2048]{3,2,0,1:T(8,128)S(1)} %add_bitcast_fusion.11) | copy-start | bytes 1572868
  63.0 1.2 copy-start.7
  63.0 1.4 copy-start.8
  63.0 1.4 copy-start.10
  63.0 1.4 copy-start.11
  63.7 1.6 %copy-start = (f32[8,1,8,2048]{3,2,0,1:T(8,128)}, f32[8,1,8,2048]{3,2,0,1:T(8,128)S(1)}, u32[]{:S(2)}) copy-start(f32[8,1,8,2048]{3,2,0,1:T(8,128)S(1)} %add_bitcast_fusion.10) | copy-start | bytes 1572868
  64.4 15.1 %copy-start.12 = (f32[4,8,128]{2,1,0:T(8,128)S(1)}, f32[4,8,128]{2,1,0:T(8,128)}, u32[]{:S(2)}) copy-start(f32[4,8,128]{2,1,0:T(8,128)} %get-tuple-element.92) | copy-start | bytes 49156
  65.0 0.8 copy-start.1
  65.8 23.2 %collective-permute-start.2 = (f32[8,3,1,2048]{3,2,0,1:T(1,128)S(1)}, f32[8,3,1,2048]{3,2,0,1:T(1,128)S(1)}, u32[]{:S(2)}, u32[]{:S(2)}) collective-permute-start(f32[8,3,1,2048]{3,2,0,1:T(1,128)S(1)} %get-tuple-element.21), channel_id=1, source_target_pairs={{0,1},{1,2},{2,3},{3,4},{4,5},{5,6},{6,7},{7,8},{8,9},{9,10},{10,1... | collective-permute-start | bytes 589832 | tf_op jit(solution)/shard_map/ppermute | solution.py:37
  67.7 21.3 %collective-permute-start.3 = (f32[8,3,1,2048]{3,2,0,1:T(1,128)S(1)}, f32[8,3,1,2048]{3,2,0,1:T(1,128)S(1)}, u32[]{:S(2)}, u32[]{:S(2)}) collective-permute-start(f32[8,3,1,2048]{3,2,0,1:T(1,128)S(1)} %get-tuple-element.22), channel_id=1, source_target_pairs={{1,0},{2,1},{3,2},{4,3},{5,4},{6,5},{7,6},{8,7},{9,8},{10,9},{11,1... | collective-permute-start | bytes 589832 | tf_op jit(solution)/shard_map/ppermute | solution.py:38
  80.2 30.1 %all-to-all-start.2 = ((f32[16,4,8,128]{3,2,1,0:T(8,128)}), f32[16,4,8,128]{3,2,1,0:T(8,128)S(1)}, u32[]{:S(2)}, u32[]{:S(2)}) async-start(f32[16,4,8,128]{3,2,1,0:T(8,128)} %broadcast_in_dim.37), calls=%async_computation.2 | async-start | bytes 524288 | tf_op jit(solution)/shard_map/all_to_all | solution.py:21
  94.3 23.2 %collective-permute-start.4 = (f32[8,3,1,2048]{3,2,0,1:T(1,128)S(1)}, f32[8,3,1,2048]{3,2,0,1:T(1,128)S(1)}, u32[]{:S(2)}, u32[]{:S(2)}) collective-permute-start(f32[8,3,1,2048]{3,2,0,1:T(1,128)S(1)} %get-tuple-element.19), channel_id=1, source_target_pairs={{0,1},{1,2},{2,3},{3,4},{4,5},{5,6},{6,7},{7,8},{8,9},{9,10},{10,1... | collective-permute-start | bytes 589832 | tf_op jit(solution)/shard_map/ppermute | solution.py:37
  96.2 21.3 %collective-permute-start.5 = (f32[8,3,1,2048]{3,2,0,1:T(1,128)S(1)}, f32[8,3,1,2048]{3,2,0,1:T(1,128)S(1)}, u32[]{:S(2)}, u32[]{:S(2)}) collective-permute-start(f32[8,3,1,2048]{3,2,0,1:T(1,128)S(1)} %get-tuple-element.20), channel_id=1, source_target_pairs={{1,0},{2,1},{3,2},{4,3},{5,4},{6,5},{7,6},{8,7},{9,8},{10,9},{11,1... | collective-permute-start | bytes 589832 | tf_op jit(solution)/shard_map/ppermute | solution.py:38
  111.1 27.7 %all-to-all-start.3 = ((f32[16,4,8,128]{3,2,1,0:T(8,128)}), f32[16,4,8,128]{3,2,1,0:T(8,128)S(1)}, u32[]{:S(2)}, u32[]{:S(2)}) async-start(f32[16,4,8,128]{3,2,1,0:T(8,128)} %broadcast_in_dim.39), calls=%async_computation.3 | async-start | bytes 524288 | tf_op jit(solution)/shard_map/all_to_all | solution.py:21
  121.4 17.4 %collective-permute-start.6 = (f32[8,3,1,2048]{3,2,0,1:T(1,128)S(1)}, f32[8,3,1,2048]{3,2,0,1:T(1,128)S(1)}, u32[]{:S(2)}, u32[]{:S(2)}) collective-permute-start(f32[8,3,1,2048]{3,2,0,1:T(1,128)S(1)} %get-tuple-element.17), channel_id=1, source_target_pairs={{0,1},{1,2},{2,3},{3,4},{4,5},{5,6},{6,7},{7,8},{8,9},{9,10},{10,1... | collective-permute-start | bytes 589832 | tf_op jit(solution)/shard_map/ppermute | solution.py:37
  123.3 15.5 %collective-permute-start.7 = (f32[8,3,1,2048]{3,2,0,1:T(1,128)S(1)}, f32[8,3,1,2048]{3,2,0,1:T(1,128)S(1)}, u32[]{:S(2)}, u32[]{:S(2)}) collective-permute-start(f32[8,3,1,2048]{3,2,0,1:T(1,128)S(1)} %get-tuple-element.18), channel_id=1, source_target_pairs={{1,0},{2,1},{3,2},{4,3},{5,4},{6,5},{7,6},{8,7},{9,8},{10,9},{11,1... | collective-permute-start | bytes 589832 | tf_op jit(solution)/shard_map/ppermute | solution.py:38
where the time goes:
time: 145 us; the launch traced here: 144 us
  starting transfers between devices  66.9 us (46%)
  waiting for transfers between devices  43.5 us (30%)
  other arithmetic  18.4 us (13%)
  local copies, waits for them, and re-layouts  14.5 us (10%)
    all_to_all x4, waiting for transfers between devices, sent_to_all(): lax.all_to_all(jnp.broadcast_to(shard[None], (count, *shard.shape)), axis...  43.5 us
    all_to_all x4, starting transfers between devices, sent_to_all(): lax.all_to_all(jnp.broadcast_to(shard[None], (count, *shard.shape)), axis...  37.3 us
    ppermute x4, starting transfers between devices, extended(): after = lax.ppermute(leading, axis, down)  20.7 us
    another operation x13, other arithmetic, advance(): return jnp.stack([new_height, new_zonal, new_north], axis=-3)  10 us
    ppermute x4, starting transfers between devices, extended(): before = lax.ppermute(last, axis, up)  8.95 us
    slice x22, local copies, waits for them, and re-layouts, lon_diff(): return 0.5 * (jnp.roll(field, -1, axis=-1) - jnp.roll(field, 1, axis=-1))  6.16 us
    concatenate x4, other arithmetic, extended(): shard = jnp.concatenate([before, shard, after], axis=dim)  4.92 us
    broadcast_in_dim x4, local copies, waits for them, and re-layouts, sent_to_all(): jnp.broadcast_to(shard[None], (count, *shard.shape))  3.63 us
  transfers between devices with their start and end apart: 12, of which 4 were waited for; matrix products, arithmetic and copies ran while one was open for 16% of the time, Pallas kernels for 0%

commit v1 on v0

v1 whole, which is shorter than its diff:
```python
import jax
import jax.numpy as jnp
from jax import lax
from jax.experimental import pallas as pl
from jax.experimental.pallas import tpu as pltpu
from jax.sharding import Mesh, PartitionSpec as P

STEPS = 4
HALO = 4
LANES = 128

time_step = 0.2
viscosity = 0.05

KEEP = 1.0 - 4.0 * time_step * viscosity
SPREAD = time_step * viscosity / KEEP
SLOPE = time_step / (2.0 * KEEP)
HEIGHT = 2.0 * KEEP / time_step

VMEM = pl.BlockSpec(memory_space=pltpu.VMEM)
SMEM = pl.BlockSpec(memory_space=pltpu.SMEM)


def split_rows(state_ref, low_ref, high_ref):
    fields, rows, lon = state_ref.shape[1:]
    half = rows // 2

    for field in range(fields):

        @pl.loop(0, lon // LANES)
        def _(tile):
            lanes = pl.ds(pl.multiple_of(tile * LANES, LANES), LANES)
            block = jnp.swapaxes(state_ref[:, field, :, lanes], 0, 1)
            if field == 0:
                block = block * (1.0 / HEIGHT)
            low_ref[field, :, :, lanes] = block[:half]
            high_ref[field, :, :, lanes] = block[half:]


def rows_first(state):
    vectors, fields, rows, lon = state.shape
    half = jax.ShapeDtypeStruct((fields, rows // 2, vectors, lon), state.dtype)
    return pl.pallas_call(
        split_rows,
        out_shape=(half, half),
        in_specs=[VMEM],
        out_specs=(VMEM, VMEM),
        compiler_params=pltpu.CompilerParams(vmem_limit_bytes=40 << 20),
    )(state)


def step_row(source, target, plus, minus, raw, moment, row, crow, tiles, edge):
    def at(field, r, tile):
        return source[field, r, :, pl.ds(tile * LANES, LANES)]

    first_lane, last_lane = edge
    held = {}

    def turned(field, tile):
        tile %= tiles
        if (field, tile) not in held:
            value = at(field, row, tile)
            held[field, tile] = (
                value,
                pltpu.roll(value, 1, 1),
                pltpu.roll(value, LANES - 1, 1),
            )
        return held[field, tile]

    def coefficient(ref, tile, channel):
        line = ref[tile, crow, pl.ds(moment * 4 + channel, 1), :]
        return jnp.broadcast_to(line, (8, LANES))

    for tile in range(tiles):
        middle, west, east, south, north = ([], [], [], [], [])
        for field in range(3):
            value, right, left = turned(field, tile)
            middle.append(value)
            west.append(jnp.where(first_lane, turned(field, tile - 1)[1], right))
            east.append(jnp.where(last_lane, turned(field, tile + 1)[2], left))
            south.append(at(field, row - 1, tile))
            north.append(at(field, row + 1, tile))
        to_east = coefficient(plus, tile, 0)
        to_west = coefficient(minus, tile, 0)
        to_north = coefficient(plus, tile, 1)
        to_south = coefficient(minus, tile, 1)
        turn = coefficient(raw, tile, 2)
        depth = coefficient(raw, tile, 3)
        new = [
            (middle[f] + to_east * east[f])
            + (to_west * west[f] + to_north * north[f])
            + to_south * south[f]
            for f in range(3)
        ]
        new[0] = new[0] + depth * ((east[1] - west[1]) + (north[2] - south[2]))
        new[1] = new[1] + (turn * middle[2] - (east[0] - west[0]))
        new[2] = new[2] - (turn * middle[1] + (north[0] - south[0]))
        for field in range(3):
            target(field, tile, new[field])


def advance_all(
    lat_ref, low_ref, high_ref, below_ref, above_ref, own_ref, cbelow_ref, cabove_ref,
    out_ref, first, second, last, raw, plus, minus, sems
):
    tiles = raw.shape[0]
    rows = out_ref.shape[2]
    half = rows // 2
    copies = [
        pltpu.make_async_copy(ref, first.at[:, pl.ds(start, count)], sems.at[k])
        for k, (ref, start, count) in enumerate(
            [
                (below_ref, 0, HALO),
                (low_ref, HALO, half),
                (high_ref, HALO + half, half),
                (above_ref, HALO + rows, HALO),
            ]
        )
    ]
    for copy in copies:
        copy.start()

    second[:, HALO - 1] = jnp.zeros_like(second[:, HALO - 1])
    second[:, HALO + rows] = jnp.zeros_like(second[:, HALO + rows])

    @pl.loop(0, tiles)
    def _(tile):
        def put(row, group, value):
            lines = pl.ds(group * 8, 8)
            raw[tile, row, lines, :] = value
            plus[tile, row, lines, :] = SPREAD + value
            minus[tile, row, lines, :] = SPREAD - value

        core, rest = (tile % 2, tile // 2)
        for row in range(rows):
            for group in range(2):
                put(3 + row, group, own_ref[core, rest, row, pl.ds(group * 8, 8), :])
        for place, (row, group) in enumerate([(0, 0), (1, 0), (2, 0), (2, 1)]):
            put(row, group, cbelow_ref[core, rest, place])
        for place, (row, group) in enumerate([(13, 0), (12, 0), (11, 0), (11, 1)]):
            put(row, group, cabove_ref[core, rest, place])

    for copy in copies:
        copy.wait()

    lane = lax.broadcasted_iota(jnp.int32, (8, LANES), 1)
    edge = (lane == 0, lane == LANES - 1)
    buffers = [first, second]
    for moment in range(STEPS):
        source, goal = (buffers[moment % 2], buffers[(moment + 1) % 2])
        final = moment == STEPS - 1
        start = jnp.where(lat_ref[0] == 0, HALO, moment + 1)
        stop = jnp.where(lat_ref[0] == lat_ref[1] - 1, HALO + rows, HALO + rows + 3 - moment)

        @pl.loop(start, stop)
        def _(row):
            def target(field, tile, value):
                lanes = pl.ds(tile * LANES, LANES)
                if final:
                    scale = KEEP**STEPS * (HEIGHT if field == 0 else 1.0)
                    last[field, row - HALO, :, lanes] = value * scale
                else:
                    goal[field, row, :, lanes] = value

            step_row(source, target, plus, minus, raw, moment, row, row - 1, tiles, edge)

    for field in range(3):

        @pl.loop(0, tiles)
        def _(tile):
            lanes = pl.ds(pl.multiple_of(tile * LANES, LANES), LANES)
            out_ref[:, field, :, lanes] = jnp.swapaxes(last[field, :, :, lanes], 0, 1)


def shards(perturbation, wind_coriolis, depth_field):
    vectors, fields, rows, lon = perturbation.shape
    tiles = lon // LANES
    count = lax.axis_size("lat")
    up = [(i, i + 1) for i in range(count - 1)]
    down = [(i + 1, i) for i in range(count - 1)]

    low, high = rows_first(perturbation)
    below = lax.ppermute(high, "lat", up)
    above = lax.ppermute(low, "lat", down)

    scales = jnp.array([-SLOPE, -SLOPE, 2.0 * SLOPE], jnp.float32)[None, :, None, None]
    packed = jnp.concatenate([wind_coriolis * scales, -SLOPE * SLOPE * depth_field[:, None]], axis=1)
    packed = packed.transpose(2, 0, 1, 3).reshape(rows, STEPS * 4, LANES)
    gathered = lax.all_gather(packed, "zh", axis=0)
    gathered = lax.all_gather(gathered, "x", axis=0)
    gathered = gathered.reshape(tiles // 2, rows, STEPS * 4, LANES)
    gathered = lax.all_gather(gathered, "core", axis=0)

    def picked(order):
        return jnp.stack([gathered[:, :, row, group * 8 : group * 8 + 8] for row, group in order], axis=2)

    cbelow = lax.ppermute(picked([(5, 0), (6, 0), (7, 0), (7, 1)]), "lat", up)
    cabove = lax.ppermute(picked([(2, 0), (1, 0), (0, 0), (0, 1)]), "lat", down)

    where = jnp.stack([lax.axis_index("lat"), jnp.int32(count)]).astype(jnp.int32)
    anywhere = pl.BlockSpec(memory_space=pl.ANY)
    table = pltpu.VMEM((tiles, rows + 6, STEPS * 4, LANES), jnp.float32)
    band = pltpu.VMEM((fields, rows + 2 * HALO, vectors, lon), jnp.float32)
    return pl.pallas_call(
        advance_all,
        out_shape=jax.ShapeDtypeStruct(perturbation.shape, perturbation.dtype),
        in_specs=[SMEM] + [anywhere] * 4 + [VMEM] * 3,
        out_specs=VMEM,
        scratch_shapes=[
            band,
            band,
            pltpu.VMEM((fields, rows, vectors, lon), jnp.float32),
            table,
            table,
            table,
            pltpu.SemaphoreType.DMA((4,)),
        ],
        compiler_params=pltpu.CompilerParams(vmem_limit_bytes=40 << 20),
    )(where, low, high, below, above, gathered, cbelow, cabove)


def solution(mesh):
    grid = Mesh(
        mesh.devices.reshape(mesh.shape["vec"] // 4, 2, 2, mesh.shape["lat"]), ("x", "zh", "core", "lat")
    )
    vec = ("x", "zh", "core")
    placed = (P(vec, None, "lat", None), P(None, None, "lat", vec), P(None, "lat", vec))
    return jax.shard_map(
        shards, mesh=grid, in_specs=placed, out_specs=P(vec, None, "lat", None), check_vma=False
    )
```

time: 145 us -> 101 us (0.70)
  the two profiles are of different devices: /device:TPU:33 before, /device:TPU:120 now
where the time goes in v1:
time: 101 us; the launch traced here: 100 us
  blocking collectives  30.5 us (30%)
  waiting for transfers between devices  23.4 us (23%)
  starting transfers between devices  15.7 us (16%)
  between operations  13.5 us (13%)
  Pallas kernels  12.6 us (12%)
  other arithmetic  2.53 us (3%)
  local copies, waits for them, and re-layouts  2.06 us (2%)
    all_gather x1, blocking collectives, shards(): gathered = lax.all_gather(packed, 'zh', axis=0)  16.6 us
    all_gather x1, blocking collectives, shards(): gathered = lax.all_gather(gathered, 'x', axis=0)  13.9 us
    pallas_call x1, Pallas kernels, shards(): pl.pallas_call(advance_all, out_shape=jax.ShapeDtypeStruct(perturbation.s...  11.9 us
    all_gather x1, waiting for transfers between devices, shards(): gathered = lax.all_gather(gathered, 'core', axis=0)  11.7 us
    ppermute x1, waiting for transfers between devices, shards(): cabove = lax.ppermute(picked([(2, 0), (1, 0), (0, 0), (0, 1)]), 'lat', down)  8.36 us
    ppermute x1, starting transfers between devices, shards(): below = lax.ppermute(high, 'lat', up)  6.51 us
    ppermute x1, starting transfers between devices, shards(): cbelow = lax.ppermute(picked([(5, 0), (6, 0), (7, 0), (7, 1)]), 'lat', up)  4.6 us
    ppermute x1, waiting for transfers between devices, shards(): cbelow = lax.ppermute(picked([(5, 0), (6, 0), (7, 0), (7, 1)]), 'lat', up)  3.29 us
  transfers between devices with their start and end apart: 5, of which 3 were waited for; matrix products, arithmetic and copies ran while one was open for 3% of the time, Pallas kernels for 1%

profile of v1, /device:TPU:120, one launch (start us, length us, event | category | flops | bytes accessed | tf_op | source)
XLA Modules:
  0.0 100.3 jit_solution(2763930781934188336)
XLA Ops:
  6.5 0.0 copy-start.1
  6.5 0.0 all-gather.4.cloned.1.call-start
  6.5 0.8 multiply_bitcast_fusion
  7.4 0.9 broadcast_multiply_fusion
  8.3 16.6 %all_gather.12 = f32[2,8,16,128]{3,2,1,0:T(8,128)S(1)} all-gather(f32[1,8,16,128]{3,2,1,0:T(8,128)S(1)} %bitcast.12), channel_id=1, replica_groups=mesh['x'=4,'zh'=2,'core'=2,'lat'=32] {'zh'}, dimensions={0}, use_global_device_ids=true | all-gather | bytes 196608 | tf_op jit(solution)/shard_map/all_gather | solution.py:189
  24.9 13.9 %all-gather = f32[8,8,16,128]{3,2,1,0:T(8,128)} all-gather(f32[2,8,16,128]{3,2,1,0:T(8,128)S(1)} %all_gather.12), channel_id=2, replica_groups=mesh['x'=4,'zh'=2,'core'=2,'lat'=32] {'x'}, dimensions={0}, use_global_device_ids=true | all-gather | bytes 655360 | tf_op jit(solution)/shard_map/all_gather | solution.py:190
  38.8 0.0 all-gather.4.cloned.1.call-update
  38.8 0.0 copy-done.1
  38.8 0.7 shard_map.46
  39.5 2.7 %collective-permute-start.1 = (f32[3,4,8,2048]{3,2,1,0:T(8,128)S(1)}, f32[3,4,8,2048]{3,2,1,0:T(8,128)}, u32[]{:S(2)}, u32[]{:S(2)}) collective-permute-start(f32[3,4,8,2048]{3,2,1,0:T(8,128)S(1)} %get-tuple-element.7.low_ref), channel_id=1, source_target_pairs={{1,0},{2,1},{3,2},{4,3},{5,4},{6,5},{7,6},{8,7},{9,8},{10,9},{11,1... | collective-permute-start | bytes 2359304 | tf_op jit(solution)/shard_map/ppermute | solution.py:184
  42.2 6.5 %collective-permute-start = (f32[3,4,8,2048]{3,2,1,0:T(8,128)S(1)}, f32[3,4,8,2048]{3,2,1,0:T(8,128)}, u32[]{:S(2)}, u32[]{:S(2)}) collective-permute-start(f32[3,4,8,2048]{3,2,1,0:T(8,128)S(1)} %get-tuple-element.8.high_ref), channel_id=1, source_target_pairs={{0,1},{1,2},{2,3},{3,4},{4,5},{5,6},{6,7},{7,8},{8,9},{9,10},{10,1... | collective-permute-start | bytes 2359304 | tf_op jit(solution)/shard_map/ppermute | solution.py:183
  48.7 11.7 %all-gather.4.cloned.1.call-done = f32[16,8,16,128]{3,2,1,0:T(8,128)} async-done(((f32[8,8,16,128]{3,2,1,0:T(8,128)}), f32[16,8,16,128]{3,2,1,0:T(8,128)}) %all-gather.4.cloned.1.call-update) | async-done | bytes 1048592 | tf_op jit(solution)/shard_map/all_gather | solution.py:192
  60.4 0.0 copy-start
  60.4 1.0 %slice.27 = f32[2,8,3,8,128]{4,3,2,1,0:T(8,128)S(1)} slice(f32[2,8,8,16,128]{4,3,2,1,0:T(8,128)} %bitcast.9), slice={[0:2], [0:8], [5:8], [0:8], [0:128]} | slice | bytes 393216 | tf_op jit(solution)/shard_map/slice | solution.py:195
  61.4 1.0 fusion
  62.5 4.6 %collective-permute-start.2 = (f32[2,8,4,8,128]{4,3,2,1,0:T(8,128)S(1)}, f32[2,8,4,8,128]{4,3,2,1,0:T(8,128)S(1)}, u32[]{:S(2)}, u32[]{:S(2)}) collective-permute-start(f32[2,8,4,8,128]{4,3,2,1,0:T(8,128)S(1)} %pad_maximum_fusion), channel_id=1, source_target_pairs={{0,1},{1,2},{2,3},{3,4},{4,5},{5,6},{6,7},{7,8},{8,9},{9,10},{10,1... | collective-permute-start | bytes 786440 | tf_op jit(solution)/shard_map/ppermute | solution.py:197
  67.1 0.7 pad_maximum_fusion.1
  67.8 1.9 %collective-permute-start.3 = (f32[2,8,4,8,128]{4,3,2,1,0:T(8,128)}, f32[2,8,4,8,128]{4,3,2,1,0:T(8,128)S(1)}, u32[]{:S(2)}, u32[]{:S(2)}) collective-permute-start(f32[2,8,4,8,128]{4,3,2,1,0:T(8,128)} %pad_maximum_fusion.1), channel_id=1, source_target_pairs={{1,0},{2,1},{3,2},{4,3},{5,4},{6,5},{7,6},{8,7},{9,8},{10,9},{11,1... | collective-permute-start | bytes 786440 | tf_op jit(solution)/shard_map/ppermute | solution.py:198
  69.7 0.1 pad_add_fusion.lat_ref
  69.8 0.0 collective-permute-done.1.above_ref
  69.8 0.0 collective-permute-done.below_ref
  69.8 3.3 %collective-permute-done.2.cbelow_ref = f32[2,8,4,8,128]{4,3,2,1,0:T(8,128)S(1)} collective-permute-done((f32[2,8,4,8,128]{4,3,2,1,0:T(8,128)S(1)}, f32[2,8,4,8,128]{4,3,2,1,0:T(8,128)S(1)}, u32[]{:S(2)}, u32[]{:S(2)}) %collective-permute-start.2) | collective-permute-done | bytes 262176 | tf_op jit(solution)/shard_map/ppermute | solution.py:197
  73.1 8.4 %collective-permute-done.3.cabove_ref = f32[2,8,4,8,128]{4,3,2,1,0:T(8,128)S(1)} collective-permute-done((f32[2,8,4,8,128]{4,3,2,1,0:T(8,128)}, f32[2,8,4,8,128]{4,3,2,1,0:T(8,128)S(1)}, u32[]{:S(2)}, u32[]{:S(2)}) %collective-permute-start.3) | collective-permute-done | bytes 262176 | tf_op jit(solution)/shard_map/ppermute | solution.py:198
  81.5 0.0 copy-done
  81.5 11.9 %shard_map.47 = f32[8,3,8,2048]{3,2,1,0:T(8,128)} custom-call(s32[2]{0:T(128)S(1)} %pad_add_fusion.lat_ref, f32[3,4,8,2048]{3,2,1,0:T(8,128)S(1)} %get-tuple-element.7.low_ref, f32[3,4,8,2048]{3,2,1,0:T(8,128)S(1)} %get-tuple-element.8.high_ref, f32[3,4,8,2048]{3,2,1,0:T(8,128)} %collective-permute-done.below_ref, ...), custom_call_target="tpu_custom_call" | custom-call | tf_op jit(solution)/shard_map/pallas_call | solution.py:204
  (3 shorter events, 0.0 us)
Async XLA Ops:
  6.5 32.3 %copy-start.1 = (f32[8,3,8,2048]{3,2,1,0:T(8,128)S(1)}, f32[8,3,8,2048]{3,2,1,0:T(8,128)}, u32[]{:S(2)}) copy-start(f32[8,3,8,2048]{3,2,1,0:T(8,128)} %state_ref.1) | copy-start | bytes 4718596
  6.5 53.9 %all-gather.4.cloned.1.call-start = ((), (), s32[]{:S(2)}) async-start(), calls=%async_computation | async-start | bytes 1572864 | tf_op jit(solution)/shard_map/all_gather | solution.py:192
  39.5 30.3 %collective-permute-start.1 = (f32[3,4,8,2048]{3,2,1,0:T(8,128)S(1)}, f32[3,4,8,2048]{3,2,1,0:T(8,128)}, u32[]{:S(2)}, u32[]{:S(2)}) collective-permute-start(f32[3,4,8,2048]{3,2,1,0:T(8,128)S(1)} %get-tuple-element.7.low_ref), channel_id=1, source_target_pairs={{1,0},{2,1},{3,2},{4,3},{5,4},{6,5},{7,6},{8,7},{9,8},{10,9},{11,1... | collective-permute-start | bytes 2359304 | tf_op jit(solution)/shard_map/ppermute | solution.py:184
  42.2 27.6 %collective-permute-start = (f32[3,4,8,2048]{3,2,1,0:T(8,128)S(1)}, f32[3,4,8,2048]{3,2,1,0:T(8,128)}, u32[]{:S(2)}, u32[]{:S(2)}) collective-permute-start(f32[3,4,8,2048]{3,2,1,0:T(8,128)S(1)} %get-tuple-element.8.high_ref), channel_id=1, source_target_pairs={{0,1},{1,2},{2,3},{3,4},{4,5},{5,6},{6,7},{7,8},{8,9},{9,10},{10,1... | collective-permute-start | bytes 2359304 | tf_op jit(solution)/shard_map/ppermute | solution.py:183
  60.4 21.1 %copy-start = (f32[16,8,16,128]{3,2,1,0:T(8,128)S(1)}, f32[16,8,16,128]{3,2,1,0:T(8,128)}, u32[]{:S(2)}) copy-start(f32[16,8,16,128]{3,2,1,0:T(8,128)} %all-gather.4.cloned.1.call-done) | copy-start | bytes 3145732
  62.5 10.6 %collective-permute-start.2 = (f32[2,8,4,8,128]{4,3,2,1,0:T(8,128)S(1)}, f32[2,8,4,8,128]{4,3,2,1,0:T(8,128)S(1)}, u32[]{:S(2)}, u32[]{:S(2)}) collective-permute-start(f32[2,8,4,8,128]{4,3,2,1,0:T(8,128)S(1)} %pad_maximum_fusion), channel_id=1, source_target_pairs={{0,1},{1,2},{2,3},{3,4},{4,5},{5,6},{6,7},{7,8},{8,9},{9,10},{10,1... | collective-permute-start | bytes 786440 | tf_op jit(solution)/shard_map/ppermute | solution.py:197
  67.8 13.6 %collective-permute-start.3 = (f32[2,8,4,8,128]{4,3,2,1,0:T(8,128)}, f32[2,8,4,8,128]{4,3,2,1,0:T(8,128)S(1)}, u32[]{:S(2)}, u32[]{:S(2)}) collective-permute-start(f32[2,8,4,8,128]{4,3,2,1,0:T(8,128)} %pad_maximum_fusion.1), channel_id=1, source_target_pairs={{1,0},{2,1},{3,2},{4,3},{5,4},{6,5},{7,6},{8,7},{9,8},{10,9},{11,1... | collective-permute-start | bytes 786440 | tf_op jit(solution)/shard_map/ppermute | solution.py:198
Sparse Core Ops, SparseCore 0:
  38.9 21.4 all-gather.3

commit v2 on v1

--- a/solution.py
+++ b/solution.py
@@ -19,6 +19,10 @@
 
 VMEM = pl.BlockSpec(memory_space=pltpu.VMEM)
 SMEM = pl.BlockSpec(memory_space=pltpu.SMEM)
+
+
+def room(mebibytes):
+    return pltpu.CompilerParams(vmem_limit_bytes=mebibytes << 20)
 
 
 def split_rows(state_ref, low_ref, high_ref):
@@ -45,8 +49,30 @@
         out_shape=(half, half),
         in_specs=[VMEM],
         out_specs=(VMEM, VMEM),
-        compiler_params=pltpu.CompilerParams(vmem_limit_bytes=40 << 20),
+        compiler_params=room(8),
     )(state)
+
+
+def pack(wind_ref, depth_ref, out_ref):
+    for pair in range(STEPS // 2):
+        planes = []
+        for moment in (2 * pair, 2 * pair + 1):
+            planes += [wind_ref[moment, 0] * -SLOPE, wind_ref[moment, 1] * -SLOPE]
+            planes += [wind_ref[moment, 2] * (2.0 * SLOPE), depth_ref[moment] * (-SLOPE * SLOPE)]
+        out_ref[:, pl.ds(8 * pair, 8), :] = jnp.swapaxes(jnp.stack(planes), 0, 1)
+
+
+def pick_halo(mine_ref, other_ref, up_ref, down_ref):
+    for core, gathered in enumerate((mine_ref, other_ref)):
+
+        @pl.loop(0, gathered.shape[0])
+        def _(quad):
+            for side in range(2):
+                for out, far, mid, near in ((up_ref, 5, 6, 7), (down_ref, 2, 1, 0)):
+                    out[core, quad, side, 0] = gathered[quad, side, mid, :8]
+                    out[core, quad, side, 1] = gathered[quad, side, near, :8]
+                    out[core, quad, side, 2, :4] = gathered[quad, side, far, :4]
+                    out[core, quad, side, 2, 4:] = gathered[quad, side, near, 8:12]
 
 
 def step_row(source, target, plus, minus, raw, moment, row, crow, tiles, edge):
@@ -96,11 +122,11 @@
         new[1] = new[1] + (turn * middle[2] - (east[0] - west[0]))
         new[2] = new[2] - (turn * middle[1] + (north[0] - south[0]))
         for field in range(3):
-            target(field, tile, new[field])
+            target(field, row, tile, new[field])
 
 
 def advance_all(
-    lat_ref, low_ref, high_ref, below_ref, above_ref, own_ref, cbelow_ref, cabove_ref,
+    place_ref, low_ref, high_ref, below_ref, above_ref, mine_ref, other_ref, cbelow_ref, cabove_ref,
     out_ref, first, second, last, raw, plus, minus, sems
 ):
     tiles = raw.shape[0]
@@ -120,25 +146,26 @@
     for copy in copies:
         copy.start()
 
-    second[:, HALO - 1] = jnp.zeros_like(second[:, HALO - 1])
-    second[:, HALO + rows] = jnp.zeros_like(second[:, HALO + rows])
-
-    @pl.loop(0, tiles)
-    def _(tile):
-        def put(row, group, value):
-            lines = pl.ds(group * 8, 8)
-            raw[tile, row, lines, :] = value
-            plus[tile, row, lines, :] = SPREAD + value
-            minus[tile, row, lines, :] = SPREAD - value
-
-        core, rest = (tile % 2, tile // 2)
-        for row in range(rows):
-            for group in range(2):
-                put(3 + row, group, own_ref[core, rest, row, pl.ds(group * 8, 8), :])
-        for place, (row, group) in enumerate([(0, 0), (1, 0), (2, 0), (2, 1)]):
-            put(row, group, cbelow_ref[core, rest, place])
-        for place, (row, group) in enumerate([(13, 0), (12, 0), (11, 0), (11, 1)]):
-            put(row, group, cabove_ref[core, rest, place])
+    @pl.loop(0, tiles // 4)
+    def _(quad):
+        for core, gathered in enumerate((mine_ref, other_ref)):
+            for side in range(2):
+                tile = quad * 4 + (side ^ place_ref[2]) * 2 + (core ^ place_ref[3])
+
+                def put(row, line, value):
+                    lines = pl.ds(line, value.shape[0])
+                    raw[tile, row, lines, :] = value
+                    plus[tile, row, lines, :] = SPREAD + value
+                    minus[tile, row, lines, :] = SPREAD - value
+
+                for row in range(rows):
+                    for line in (0, 8):
+                        put(3 + row, line, gathered[quad, side, row, pl.ds(line, 8), :])
+                for halo, far, mid, near in ((cbelow_ref, 0, 1, 2), (cabove_ref, 13, 12, 11)):
+                    put(mid, 0, halo[core, quad, side, 0])
+                    put(near, 0, halo[core, quad, side, 1])
+                    put(far, 0, halo[core, quad, side, 2, :4])
+                    put(near, 8, halo[core, quad, side, 2, 4:])
 
     for copy in copies:
         copy.wait()
@@ -149,12 +176,10 @@
     for moment in range(STEPS):
         source, goal = (buffers[moment % 2], buffers[(moment + 1) % 2])
         final = moment == STEPS - 1
-        start = jnp.where(lat_ref[0] == 0, HALO, moment + 1)
-        stop = jnp.where(lat_ref[0] == lat_ref[1] - 1, HALO + rows, HALO + rows + 3 - moment)
-
-        @pl.loop(start, stop)
-        def _(row):
-            def target(field, tile, value):
+
+        @pl.loop(moment + 1, HALO + rows + 3 - moment, step=2)
+        def _(pair):
+            def target(field, row, tile, value):
                 lanes = pl.ds(tile * LANES, LANES)
                 if final:
                     scale = KEEP**STEPS * (HEIGHT if field == 0 else 1.0)
@@ -162,7 +187,18 @@
                 else:
                     goal[field, row, :, lanes] = value
 
-            step_row(source, target, plus, minus, raw, moment, row, row - 1, tiles, edge)
+            for row in (pair, pair + 1):
+                step_row(source, target, plus, minus, raw, moment, row, row - 1, tiles, edge)
+
+        if not final:
+
+            @pl.when(place_ref[0] == 0)
+            def _():
+                goal[:, HALO - 1] = jnp.zeros_like(goal[:, HALO - 1])
+
+            @pl.when(place_ref[0] == place_ref[1] - 1)
+            def _():
+                goal[:, HALO + rows] = jnp.zeros_like(goal[:, HALO + rows])
 
     for field in range(3):
 
@@ -183,28 +219,37 @@
     below = lax.ppermute(high, "lat", up)
     above = lax.ppermute(low, "lat", down)
 
-    scales = jnp.array([-SLOPE, -SLOPE, 2.0 * SLOPE], jnp.float32)[None, :, None, None]
-    packed = jnp.concatenate([wind_coriolis * scales, -SLOPE * SLOPE * depth_field[:, None]], axis=1)
-    packed = packed.transpose(2, 0, 1, 3).reshape(rows, STEPS * 4, LANES)
-    gathered = lax.all_gather(packed, "zh", axis=0)
-    gathered = lax.all_gather(gathered, "x", axis=0)
-    gathered = gathered.reshape(tiles // 2, rows, STEPS * 4, LANES)
-    gathered = lax.all_gather(gathered, "core", axis=0)
-
-    def picked(order):
-        return jnp.stack([gathered[:, :, row, group * 8 : group * 8 + 8] for row, group in order], axis=2)
-
-    cbelow = lax.ppermute(picked([(5, 0), (6, 0), (7, 0), (7, 1)]), "lat", up)
-    cabove = lax.ppermute(picked([(2, 0), (1, 0), (0, 0), (0, 1)]), "lat", down)
-
-    where = jnp.stack([lax.axis_index("lat"), jnp.int32(count)]).astype(jnp.int32)
+    packed = pl.pallas_call(
+        pack,
+        out_shape=jax.ShapeDtypeStruct((rows, STEPS * 4, LANES), jnp.float32),
+        in_specs=[VMEM] * 2,
+        out_specs=VMEM,
+        compiler_params=room(4),
+    )(wind_coriolis, depth_field)
+    swap = [(0, 1), (1, 0)]
+    mine = jnp.stack([packed, lax.ppermute(packed, "zh", swap)])
+    mine = lax.all_gather(mine, "x", axis=0)
+    other = lax.ppermute(mine, "core", swap)
+    picked = jax.ShapeDtypeStruct((2, tiles // 4, 2, 3, 8, LANES), jnp.float32)
+    to_up, to_down = pl.pallas_call(
+        pick_halo,
+        out_shape=(picked, picked),
+        in_specs=[VMEM] * 2,
+        out_specs=(VMEM, VMEM),
+        compiler_params=room(4),
+    )(mine, other)
+    cbelow = lax.ppermute(to_up, "lat", up)
+    cabove = lax.ppermute(to_down, "lat", down)
+
+    place = [lax.axis_index("lat"), count, lax.axis_index("zh"), lax.axis_index("core")]
+    place = jnp.stack([jnp.int32(number) for number in place])
     anywhere = pl.BlockSpec(memory_space=pl.ANY)
     table = pltpu.VMEM((tiles, rows + 6, STEPS * 4, LANES), jnp.float32)
     band = pltpu.VMEM((fields, rows + 2 * HALO, vectors, lon), jnp.float32)
     return pl.pallas_call(
         advance_all,
         out_shape=jax.ShapeDtypeStruct(perturbation.shape, perturbation.dtype),
-        in_specs=[SMEM] + [anywhere] * 4 + [VMEM] * 3,
+        in_specs=[SMEM] + [anywhere] * 4 + [VMEM] * 4,
         out_specs=VMEM,
         scratch_shapes=[
             band,
@@ -215,8 +260,8 @@
             table,
             pltpu.SemaphoreType.DMA((4,)),
         ],
-        compiler_params=pltpu.CompilerParams(vmem_limit_bytes=40 << 20),
-    )(where, low, high, below, above, gathered, cbelow, cabove)
+        compiler_params=room(24),
+    )(place, low, high, below, above, mine, other, cbelow, cabove)
 
 
 def solution(mesh):

time: 101 us -> 69.3 us (0.69)
  the two profiles are of different devices: /device:TPU:120 before, /device:TPU:26 now
where the time goes in v2:
time: 69.3 us; the launch traced here: 68.9 us
  starting transfers between devices  31.4 us (45%)
  blocking collectives  13.5 us (19%)
  Pallas kernels  11.7 us (17%)
  waiting for transfers between devices  9.13 us (13%)
  local copies, waits for them, and re-layouts  2.92 us (4%)
    ppermute x1, starting transfers between devices, shards(): mine = jnp.stack([packed, lax.ppermute(packed, 'zh', swap)])  15.7 us
    all_gather x1, blocking collectives, shards(): mine = lax.all_gather(mine, 'x', axis=0)  13.5 us
    pallas_call x1, Pallas kernels, shards(): pl.pallas_call(advance_all, out_shape=jax.ShapeDtypeStruct(perturbation.s...  10.2 us
    ppermute x1, starting transfers between devices, shards(): below = lax.ppermute(high, 'lat', up)  5.3 us
    ppermute x1, waiting for transfers between devices, shards(): cabove = lax.ppermute(to_down, 'lat', down)  4.04 us
    ppermute x1, starting transfers between devices, shards(): cabove = lax.ppermute(to_down, 'lat', down)  3.92 us
    ppermute x1, waiting for transfers between devices, shards(): cbelow = lax.ppermute(to_up, 'lat', up)  3.21 us
    unnamed x6, local copies, waits for them, and re-layouts  2.92 us
  transfers between devices with their start and end apart: 6, of which 3 were waited for; matrix products, arithmetic and copies ran while one was open for 0% of the time, Pallas kernels for 2%

profile of v2, /device:TPU:26, one launch (start us, length us, event | category | flops | bytes accessed | tf_op | source)
XLA Modules:
  0.0 68.9 jit_solution(15927242540490778044)
XLA Ops:
  0.0 0.0 copy-start.1
  0.0 0.8 %copy-done.1 = f32[4,3,8,128]{3,2,1,0:T(8,128)S(1)} copy-done((f32[4,3,8,128]{3,2,1,0:T(8,128)S(1)}, f32[4,3,8,128]{3,2,1,0:T(8,128)}, u32[]{:S(2)}) %copy-start.1) | copy-done | bytes 49176
  0.8 0.0 copy-start.2
  0.8 0.7 %copy-done.2 = f32[4,8,128]{2,1,0:T(8,128)S(1)} copy-done((f32[4,8,128]{2,1,0:T(8,128)S(1)}, f32[4,8,128]{2,1,0:T(8,128)}, u32[]{:S(2)}) %copy-start.2) | copy-done | bytes 16408
  1.5 15.7 %collective-permute-start.2 = (f32[8,16,128]{2,1,0:T(8,128)S(1)}, f32[8,16,128]{2,1,0:T(8,128)S(1)}, u32[]{:S(2)}, u32[]{:S(2)}) collective-permute-start(f32[8,16,128]{2,1,0:T(8,128)S(1)} %shard_map.38), channel_id=1, source_target_pairs={{0,64},{64,0},{1,65},{65,1},{2,66},{66,2},{3,67},{67,3},{4,68},{68... | collective-permute-start | bytes 196616 | tf_op jit(solution)/shard_map/ppermute | solution.py:230
  17.3 0.0 copy-start
  17.3 1.4 %copy-done = f32[8,3,8,2048]{3,2,1,0:T(8,128)S(1)} copy-done((f32[8,3,8,2048]{3,2,1,0:T(8,128)S(1)}, f32[8,3,8,2048]{3,2,1,0:T(8,128)}, u32[]{:S(2)}) %copy-start) | copy-done | bytes 1572888
  18.7 0.7 shard_map.37
  19.3 2.7 %collective-permute-start.1 = (f32[3,4,8,2048]{3,2,1,0:T(8,128)S(1)}, f32[3,4,8,2048]{3,2,1,0:T(8,128)S(1)}, u32[]{:S(2)}, u32[]{:S(2)}) collective-permute-start(f32[3,4,8,2048]{3,2,1,0:T(8,128)S(1)} %get-tuple-element.9.low_ref), channel_id=1, source_target_pairs={{1,0},{2,1},{3,2},{4,3},{5,4},{6,5},{7,6},{8,7},{9,8},{10,9},{11,1... | collective-permute-start | bytes 2359304 | tf_op jit(solution)/shard_map/ppermute | solution.py:220
  22.0 5.3 %collective-permute-start = (f32[3,4,8,2048]{3,2,1,0:T(8,128)S(1)}, f32[3,4,8,2048]{3,2,1,0:T(8,128)}, u32[]{:S(2)}, u32[]{:S(2)}) collective-permute-start(f32[3,4,8,2048]{3,2,1,0:T(8,128)S(1)} %get-tuple-element.10.high_ref), channel_id=1, source_target_pairs={{0,1},{1,2},{2,3},{3,4},{4,5},{5,6},{6,7},{7,8},{8,9},{9,10},{10,1... | collective-permute-start | bytes 2359304 | tf_op jit(solution)/shard_map/ppermute | solution.py:219
  27.3 0.0 collective-permute-done.2
  27.3 13.5 %all-gather = f32[8,8,16,128]{3,2,1,0:T(8,128)S(1)} all-gather(f32[2,8,16,128]{3,2,1,0:T(8,128)S(1)} %pad_maximum_fusion), channel_id=2, replica_groups=mesh['x'=4,'zh'=2,'core'=2,'lat'=32] {'x'}, dimensions={0}, use_global_device_ids=true | all-gather | bytes 655360 | tf_op jit(solution)/shard_map/all_gather | solution.py:231
  40.9 1.9 %collective-permute-start.3 = (f32[4,2,8,16,128]{4,3,2,1,0:T(8,128)S(1)}, f32[4,2,8,16,128]{4,3,2,1,0:T(8,128)S(1)}, u32[]{:S(2)}, u32[]{:S(2)}) collective-permute-start(f32[4,2,8,16,128]{4,3,2,1,0:T(8,128)S(1)} %bitcast.6), channel_id=1, source_target_pairs={{0,32},{32,0},{1,33},{33,1},{2,34},{34,2},{3,35},{35,3},{4,36},{36... | collective-permute-start | bytes 1572872 | tf_op jit(solution)/shard_map/ppermute | solution.py:232
  42.8 1.9 %collective-permute-done.3.other_ref = f32[4,2,8,16,128]{4,3,2,1,0:T(8,128)S(1)} collective-permute-done((f32[4,2,8,16,128]{4,3,2,1,0:T(8,128)S(1)}, f32[4,2,8,16,128]{4,3,2,1,0:T(8,128)S(1)}, u32[]{:S(2)}, u32[]{:S(2)}) %collective-permute-start.3) | collective-permute-done | bytes 524320 | tf_op jit(solution)/shard_map/ppermute | solution.py:232
  44.7 0.8 %shard_map.39 = (f32[2,4,2,3,8,128]{5,4,3,2,1,0:T(8,128)}, f32[2,4,2,3,8,128]{5,4,3,2,1,0:T(8,128)}) custom-call(f32[4,2,8,16,128]{4,3,2,1,0:T(8,128)S(1)} %bitcast.7, f32[4,2,8,16,128]{4,3,2,1,0:T(8,128)S(1)} %collective-permute-done.3.other_ref), custom_call_target="tpu_custom_call" | custom-call | tf_op jit(solution)/shard_map/pallas_call | solution.py:234
  45.5 1.9 %collective-permute-start.4 = (f32[2,4,2,3,8,128]{5,4,3,2,1,0:T(8,128)}, f32[2,4,2,3,8,128]{5,4,3,2,1,0:T(8,128)}, u32[]{:S(2)}, u32[]{:S(2)}) collective-permute-start(f32[2,4,2,3,8,128]{5,4,3,2,1,0:T(8,128)} %get-tuple-element.11), channel_id=1, source_target_pairs={{0,1},{1,2},{2,3},{3,4},{4,5},{5,6},{6,7},{7,8},{8,9},{9,10},{10,1... | collective-permute-start | bytes 589832 | tf_op jit(solution)/shard_map/ppermute | solution.py:241
  47.4 3.9 %collective-permute-start.5 = (f32[2,4,2,3,8,128]{5,4,3,2,1,0:T(8,128)}, f32[2,4,2,3,8,128]{5,4,3,2,1,0:T(8,128)}, u32[]{:S(2)}, u32[]{:S(2)}) collective-permute-start(f32[2,4,2,3,8,128]{5,4,3,2,1,0:T(8,128)} %get-tuple-element.12), channel_id=1, source_target_pairs={{1,0},{2,1},{3,2},{4,3},{5,4},{6,5},{7,6},{8,7},{9,8},{10,9},{11,1... | collective-permute-start | bytes 589832 | tf_op jit(solution)/shard_map/ppermute | solution.py:242
  51.3 0.1 pad_add_fusion.place_ref
  51.4 3.2 %collective-permute-done.4.cbelow_ref = f32[2,4,2,3,8,128]{5,4,3,2,1,0:T(8,128)} collective-permute-done((f32[2,4,2,3,8,128]{5,4,3,2,1,0:T(8,128)}, f32[2,4,2,3,8,128]{5,4,3,2,1,0:T(8,128)}, u32[]{:S(2)}, u32[]{:S(2)}) %collective-permute-start.4) | collective-permute-done | bytes 196640 | tf_op jit(solution)/shard_map/ppermute | solution.py:241
  54.6 4.0 %collective-permute-done.5.cabove_ref = f32[2,4,2,3,8,128]{5,4,3,2,1,0:T(8,128)} collective-permute-done((f32[2,4,2,3,8,128]{5,4,3,2,1,0:T(8,128)}, f32[2,4,2,3,8,128]{5,4,3,2,1,0:T(8,128)}, u32[]{:S(2)}, u32[]{:S(2)}) %collective-permute-start.5) | collective-permute-done | bytes 196640 | tf_op jit(solution)/shard_map/ppermute | solution.py:242
  58.7 0.0 collective-permute-done.1.above_ref
  58.7 0.0 collective-permute-done.below_ref
  58.7 10.2 %shard_map.40 = f32[8,3,8,2048]{3,2,1,0:T(8,128)} custom-call(s32[4]{0:T(128)S(1)} %pad_add_fusion.place_ref, f32[3,4,8,2048]{3,2,1,0:T(8,128)S(1)} %get-tuple-element.9.low_ref, f32[3,4,8,2048]{3,2,1,0:T(8,128)S(1)} %get-tuple-element.10.high_ref, f32[3,4,8,2048]{3,2,1,0:T(8,128)} %collective-permute-done.below_ref, ...), custom_call_target="tpu_custom_call" | custom-call | tf_op jit(solution)/shard_map/pallas_call | solution.py:249
  (2 shorter events, 0.0 us)
Async XLA Ops:
  0.0 0.8 %copy-start.1 = (f32[4,3,8,128]{3,2,1,0:T(8,128)S(1)}, f32[4,3,8,128]{3,2,1,0:T(8,128)}, u32[]{:S(2)}) copy-start(f32[4,3,8,128]{3,2,1,0:T(8,128)} %wind_ref.1) | copy-start | bytes 147460
  0.8 0.7 %copy-start.2 = (f32[4,8,128]{2,1,0:T(8,128)S(1)}, f32[4,8,128]{2,1,0:T(8,128)}, u32[]{:S(2)}) copy-start(f32[4,8,128]{2,1,0:T(8,128)} %depth_ref.1) | copy-start | bytes 49156
  1.5 25.8 %collective-permute-start.2 = (f32[8,16,128]{2,1,0:T(8,128)S(1)}, f32[8,16,128]{2,1,0:T(8,128)S(1)}, u32[]{:S(2)}, u32[]{:S(2)}) collective-permute-start(f32[8,16,128]{2,1,0:T(8,128)S(1)} %shard_map.38), channel_id=1, source_target_pairs={{0,64},{64,0},{1,65},{65,1},{2,66},{66,2},{3,67},{67,3},{4,68},{68... | collective-permute-start | bytes 196616 | tf_op jit(solution)/shard_map/ppermute | solution.py:230
  17.3 1.4 %copy-start = (f32[8,3,8,2048]{3,2,1,0:T(8,128)S(1)}, f32[8,3,8,2048]{3,2,1,0:T(8,128)}, u32[]{:S(2)}) copy-start(f32[8,3,8,2048]{3,2,1,0:T(8,128)} %state_ref.1) | copy-start | bytes 4718596
  19.3 39.3 %collective-permute-start.1 = (f32[3,4,8,2048]{3,2,1,0:T(8,128)S(1)}, f32[3,4,8,2048]{3,2,1,0:T(8,128)S(1)}, u32[]{:S(2)}, u32[]{:S(2)}) collective-permute-start(f32[3,4,8,2048]{3,2,1,0:T(8,128)S(1)} %get-tuple-element.9.low_ref), channel_id=1, source_target_pairs={{1,0},{2,1},{3,2},{4,3},{5,4},{6,5},{7,6},{8,7},{9,8},{10,9},{11,1... | collective-permute-start | bytes 2359304 | tf_op jit(solution)/shard_map/ppermute | solution.py:220
  22.0 36.7 %collective-permute-start = (f32[3,4,8,2048]{3,2,1,0:T(8,128)S(1)}, f32[3,4,8,2048]{3,2,1,0:T(8,128)}, u32[]{:S(2)}, u32[]{:S(2)}) collective-permute-start(f32[3,4,8,2048]{3,2,1,0:T(8,128)S(1)} %get-tuple-element.10.high_ref), channel_id=1, source_target_pairs={{0,1},{1,2},{2,3},{3,4},{4,5},{5,6},{6,7},{7,8},{8,9},{9,10},{10,1... | collective-permute-start | bytes 2359304 | tf_op jit(solution)/shard_map/ppermute | solution.py:219
  40.9 3.8 %collective-permute-start.3 = (f32[4,2,8,16,128]{4,3,2,1,0:T(8,128)S(1)}, f32[4,2,8,16,128]{4,3,2,1,0:T(8,128)S(1)}, u32[]{:S(2)}, u32[]{:S(2)}) collective-permute-start(f32[4,2,8,16,128]{4,3,2,1,0:T(8,128)S(1)} %bitcast.6), channel_id=1, source_target_pairs={{0,32},{32,0},{1,33},{33,1},{2,34},{34,2},{3,35},{35,3},{4,36},{36... | collective-permute-start | bytes 1572872 | tf_op jit(solution)/shard_map/ppermute | solution.py:232
  45.5 9.1 %collective-permute-start.4 = (f32[2,4,2,3,8,128]{5,4,3,2,1,0:T(8,128)}, f32[2,4,2,3,8,128]{5,4,3,2,1,0:T(8,128)}, u32[]{:S(2)}, u32[]{:S(2)}) collective-permute-start(f32[2,4,2,3,8,128]{5,4,3,2,1,0:T(8,128)} %get-tuple-element.11), channel_id=1, source_target_pairs={{0,1},{1,2},{2,3},{3,4},{4,5},{5,6},{6,7},{7,8},{8,9},{9,10},{10,1... | collective-permute-start | bytes 589832 | tf_op jit(solution)/shard_map/ppermute | solution.py:241
  47.4 11.3 %collective-permute-start.5 = (f32[2,4,2,3,8,128]{5,4,3,2,1,0:T(8,128)}, f32[2,4,2,3,8,128]{5,4,3,2,1,0:T(8,128)}, u32[]{:S(2)}, u32[]{:S(2)}) collective-permute-start(f32[2,4,2,3,8,128]{5,4,3,2,1,0:T(8,128)} %get-tuple-element.12), channel_id=1, source_target_pairs={{1,0},{2,1},{3,2},{4,3},{5,4},{6,5},{7,6},{8,7},{9,8},{10,9},{11,1... | collective-permute-start | bytes 589832 | tf_op jit(solution)/shard_map/ppermute | solution.py:242

commit v3 on v2

--- a/solution.py
+++ b/solution.py
@@ -7,6 +7,7 @@
 
 STEPS = 4
 HALO = 4
+UNROLL = 2
 LANES = 128
 
 time_step = 0.2
@@ -53,26 +54,22 @@
     )(state)
 
 
-def pack(wind_ref, depth_ref, out_ref):
+def pack(wind_ref, depth_ref, own_ref, up_ref, down_ref):
     for pair in range(STEPS // 2):
         planes = []
         for moment in (2 * pair, 2 * pair + 1):
             planes += [wind_ref[moment, 0] * -SLOPE, wind_ref[moment, 1] * -SLOPE]
             planes += [wind_ref[moment, 2] * (2.0 * SLOPE), depth_ref[moment] * (-SLOPE * SLOPE)]
-        out_ref[:, pl.ds(8 * pair, 8), :] = jnp.swapaxes(jnp.stack(planes), 0, 1)
-
-
-def pick_halo(mine_ref, other_ref, up_ref, down_ref):
-    for core, gathered in enumerate((mine_ref, other_ref)):
-
-        @pl.loop(0, gathered.shape[0])
-        def _(quad):
-            for side in range(2):
-                for out, far, mid, near in ((up_ref, 5, 6, 7), (down_ref, 2, 1, 0)):
-                    out[core, quad, side, 0] = gathered[quad, side, mid, :8]
-                    out[core, quad, side, 1] = gathered[quad, side, near, :8]
-                    out[core, quad, side, 2, :4] = gathered[quad, side, far, :4]
-                    out[core, quad, side, 2, 4:] = gathered[quad, side, near, 8:12]
+        block = jnp.swapaxes(jnp.stack(planes), 0, 1)
+        for row in range(block.shape[0]):
+            own_ref[2 * row + pair] = block[row]
+        for out, far, mid, near in ((up_ref, 5, 6, 7), (down_ref, 2, 1, 0)):
+            if pair == 0:
+                out[0] = block[mid]
+                out[1] = block[near]
+                out[2, :4] = block[far, :4]
+            else:
+                out[2, 4:] = block[near, :4]
 
 
 def step_row(source, target, plus, minus, raw, moment, row, crow, tiles, edge):
@@ -125,26 +122,20 @@
             target(field, row, tile, new[field])
 
 
+def lay_band(below_ref, low_ref, high_ref, above_ref, band_ref):
+    for field in range(band_ref.shape[0]):
+        start = 0
+        for ref in (below_ref, low_ref, high_ref, above_ref):
+            for row in range(ref.shape[1]):
+                band_ref[field, start + row] = ref[field, row]
+            start += ref.shape[1]
+
+
 def advance_all(
-    place_ref, low_ref, high_ref, below_ref, above_ref, mine_ref, other_ref, cbelow_ref, cabove_ref,
-    out_ref, first, second, last, raw, plus, minus, sems
+    place_ref, band_ref, mine_ref, other_ref, out_ref, first, second, last, raw, plus, minus, sems
 ):
     tiles = raw.shape[0]
     rows = out_ref.shape[2]
-    half = rows // 2
-    copies = [
-        pltpu.make_async_copy(ref, first.at[:, pl.ds(start, count)], sems.at[k])
-        for k, (ref, start, count) in enumerate(
-            [
-                (below_ref, 0, HALO),
-                (low_ref, HALO, half),
-                (high_ref, HALO + half, half),
-                (above_ref, HALO + rows, HALO),
-            ]
-        )
-    ]
-    for copy in copies:
-        copy.start()
 
     @pl.loop(0, tiles // 4)
     def _(quad):
@@ -159,36 +150,44 @@
                     minus[tile, row, lines, :] = SPREAD - value
 
                 for row in range(rows):
-                    for line in (0, 8):
-                        put(3 + row, line, gathered[quad, side, row, pl.ds(line, 8), :])
-                for halo, far, mid, near in ((cbelow_ref, 0, 1, 2), (cabove_ref, 13, 12, 11)):
-                    put(mid, 0, halo[core, quad, side, 0])
-                    put(near, 0, halo[core, quad, side, 1])
-                    put(far, 0, halo[core, quad, side, 2, :4])
-                    put(near, 8, halo[core, quad, side, 2, 4:])
-
-    for copy in copies:
-        copy.wait()
+                    for pair in range(2):
+                        put(3 + row, 8 * pair, gathered[quad, side, 2 * row + pair])
+                for start, far, mid, near in ((2 * rows, 0, 1, 2), (2 * rows + 3, 13, 12, 11)):
+                    put(mid, 0, gathered[quad, side, start])
+                    put(near, 0, gathered[quad, side, start + 1])
+                    put(far, 0, gathered[quad, side, start + 2, :4])
+                    put(near, 8, gathered[quad, side, start + 2, 4:])
 
     lane = lax.broadcasted_iota(jnp.int32, (8, LANES), 1)
     edge = (lane == 0, lane == LANES - 1)
-    buffers = [first, second]
-    for moment in range(STEPS):
-        source, goal = (buffers[moment % 2], buffers[(moment + 1) % 2])
+
+    def leaving(field, row):
+        return pltpu.make_async_copy(last.at[field, row], out_ref.at[:, field, row], sems.at[field, row])
+
+    for moment, (source, goal) in enumerate([(band_ref, first), (first, second), (second, first), (first, last)]):
         final = moment == STEPS - 1
 
-        @pl.loop(moment + 1, HALO + rows + 3 - moment, step=2)
-        def _(pair):
+        def rows_of(start, count):
             def target(field, row, tile, value):
                 lanes = pl.ds(tile * LANES, LANES)
                 if final:
                     scale = KEEP**STEPS * (HEIGHT if field == 0 else 1.0)
-                    last[field, row - HALO, :, lanes] = value * scale
+                    goal[field, row - HALO, :, lanes] = value * scale
                 else:
                     goal[field, row, :, lanes] = value
 
-            for row in (pair, pair + 1):
+            for row in range(count):
+                row += start
                 step_row(source, target, plus, minus, raw, moment, row, row - 1, tiles, edge)
+                if final:
+                    for field in range(3):
+                        leaving(field, row - HALO).start()
+
+        begin, count = (moment + 1, rows + 2 * (STEPS - 1 - moment))
+
+        @pl.loop(begin, begin + count, step=UNROLL)
+        def _(row):
+            rows_of(row, UNROLL)
 
         if not final:
 
@@ -200,12 +199,10 @@
             def _():
                 goal[:, HALO + rows] = jnp.zeros_like(goal[:, HALO + rows])
 
-    for field in range(3):
-
-        @pl.loop(0, tiles)
-        def _(tile):
-            lanes = pl.ds(pl.multiple_of(tile * LANES, LANES), LANES)
-            out_ref[:, field, :, lanes] = jnp.swapaxes(last[field, :, :, lanes], 0, 1)
+    @pl.loop(0, rows)
+    def _(row):
+        for field in range(3):
+            leaving(field, row).wait()
 
 
 def shards(perturbation, wind_coriolis, depth_field):
@@ -219,49 +216,48 @@
     below = lax.ppermute(high, "lat", up)
     above = lax.ppermute(low, "lat", down)
 
-    packed = pl.pallas_call(
+    few = jax.ShapeDtypeStruct((3, 8, LANES), jnp.float32)
+    own, to_up, to_down = pl.pallas_call(
         pack,
-        out_shape=jax.ShapeDtypeStruct((rows, STEPS * 4, LANES), jnp.float32),
+        out_shape=(jax.ShapeDtypeStruct((2 * rows, 8, LANES), jnp.float32), few, few),
         in_specs=[VMEM] * 2,
-        out_specs=VMEM,
+        out_specs=(VMEM,) * 3,
         compiler_params=room(4),
     )(wind_coriolis, depth_field)
+    own = jnp.concatenate([own, lax.ppermute(to_up, "lat", up), lax.ppermute(to_down, "lat", down)])
+    own, low, high = lax.optimization_barrier((own, low, high))
     swap = [(0, 1), (1, 0)]
-    mine = jnp.stack([packed, lax.ppermute(packed, "zh", swap)])
+    mine = jnp.stack([own, lax.ppermute(own, "zh", swap)])
     mine = lax.all_gather(mine, "x", axis=0)
     other = lax.ppermute(mine, "core", swap)
-    picked = jax.ShapeDtypeStruct((2, tiles // 4, 2, 3, 8, LANES), jnp.float32)
-    to_up, to_down = pl.pallas_call(
-        pick_halo,
-        out_shape=(picked, picked),
-        in_specs=[VMEM] * 2,
-        out_specs=(VMEM, VMEM),
-        compiler_params=room(4),
-    )(mine, other)
-    cbelow = lax.ppermute(to_up, "lat", up)
-    cabove = lax.ppermute(to_down, "lat", down)
 
     place = [lax.axis_index("lat"), count, lax.axis_index("zh"), lax.axis_index("core")]
     place = jnp.stack([jnp.int32(number) for number in place])
-    anywhere = pl.BlockSpec(memory_space=pl.ANY)
     table = pltpu.VMEM((tiles, rows + 6, STEPS * 4, LANES), jnp.float32)
-    band = pltpu.VMEM((fields, rows + 2 * HALO, vectors, lon), jnp.float32)
+    band = (fields, rows + 2 * HALO, vectors, lon)
+    laid = pl.pallas_call(
+        lay_band,
+        out_shape=jax.ShapeDtypeStruct(band, jnp.float32),
+        in_specs=[VMEM] * 4,
+        out_specs=VMEM,
+        compiler_params=room(8),
+    )(below, low, high, above)
     return pl.pallas_call(
         advance_all,
         out_shape=jax.ShapeDtypeStruct(perturbation.shape, perturbation.dtype),
-        in_specs=[SMEM] + [anywhere] * 4 + [VMEM] * 4,
-        out_specs=VMEM,
+        in_specs=[SMEM] + [VMEM] * 3,
+        out_specs=pl.BlockSpec(memory_space=pl.ANY),
         scratch_shapes=[
-            band,
-            band,
+            pltpu.VMEM(band, jnp.float32),
+            pltpu.VMEM(band, jnp.float32),
             pltpu.VMEM((fields, rows, vectors, lon), jnp.float32),
             table,
             table,
             table,
-            pltpu.SemaphoreType.DMA((4,)),
+            pltpu.SemaphoreType.DMA((fields, rows)),
         ],
-        compiler_params=room(24),
-    )(place, low, high, below, above, mine, other, cbelow, cabove)
+        compiler_params=room(14),
+    )(place, laid, mine, other)
 
 
 def solution(mesh):

time: 69.3 us -> 63.6 us (0.918)
  the two profiles are of different devices: /device:TPU:26 before, /device:TPU:33 now
where the time goes in v3:
time: 63.6 us; the launch traced here: 62.7 us
  starting transfers between devices  35.2 us (55%)
  blocking collectives  12.1 us (19%)
  Pallas kernels  10.9 us (17%)
  local copies, waits for them, and re-layouts  2.92 us (5%)
  waiting for transfers between devices  1.37 us (2%)
    ppermute x1, starting transfers between devices, shards(): mine = jnp.stack([own, lax.ppermute(own, 'zh', swap)])  14.5 us
    all_gather x1, blocking collectives, shards(): mine = lax.all_gather(mine, 'x', axis=0)  12.1 us
    pallas_call x1, Pallas kernels, shards(): pl.pallas_call(advance_all, out_shape=jax.ShapeDtypeStruct(perturbation.s...  8.9 us
    ppermute x1, starting transfers between devices, shards(): other = lax.ppermute(mine, 'core', swap)  5.87 us
    ppermute x1, starting transfers between devices, shards(): above = lax.ppermute(low, 'lat', down)  5.47 us
    ppermute x1, starting transfers between devices, shards(): lax.ppermute(to_down, 'lat', down)  4.19 us
    ppermute x1, starting transfers between devices, shards(): lax.ppermute(to_up, 'lat', up)  3.2 us
    unnamed x6, local copies, waits for them, and re-layouts  2.92 us
  transfers between devices with their start and end apart: 6, of which 1 were waited for; matrix products, arithmetic and copies ran while one was open for 0% of the time, Pallas kernels for 3%

profile of v3, /device:TPU:33, one launch (start us, length us, event | category | flops | bytes accessed | tf_op | source)
XLA Modules:
  0.0 62.7 jit_solution(12254191523950888004)
XLA Ops:
  0.0 0.0 copy-start.1
  0.0 0.8 %copy-done.1 = f32[4,3,8,128]{3,2,1,0:T(8,128)S(1)} copy-done((f32[4,3,8,128]{3,2,1,0:T(8,128)S(1)}, f32[4,3,8,128]{3,2,1,0:T(8,128)}, u32[]{:S(2)}) %copy-start.1) | copy-done | bytes 49176
  0.8 0.0 copy-start.2
  0.8 0.7 %copy-done.2 = f32[4,8,128]{2,1,0:T(8,128)S(1)} copy-done((f32[4,8,128]{2,1,0:T(8,128)S(1)}, f32[4,8,128]{2,1,0:T(8,128)}, u32[]{:S(2)}) %copy-start.2) | copy-done | bytes 16408
  1.5 3.2 %collective-permute-start.1 = (f32[3,8,128]{2,1,0:T(8,128)S(1)}, f32[3,8,128]{2,1,0:T(8,128)S(1)}, u32[]{:S(2)}, u32[]{:S(2)}) collective-permute-start(f32[3,8,128]{2,1,0:T(8,128)S(1)} %get-tuple-element.15), channel_id=1, source_target_pairs={{0,1},{1,2},{2,3},{3,4},{4,5},{5,6},{6,7},{7,8},{8,9},{9,10},{10,1... | collective-permute-start | bytes 36872 | tf_op jit(solution)/shard_map/ppermute | solution.py:227
  4.8 4.2 %collective-permute-start.2 = (f32[3,8,128]{2,1,0:T(8,128)S(1)}, f32[3,8,128]{2,1,0:T(8,128)S(1)}, u32[]{:S(2)}, u32[]{:S(2)}) collective-permute-start(f32[3,8,128]{2,1,0:T(8,128)S(1)} %get-tuple-element.16), channel_id=1, source_target_pairs={{1,0},{2,1},{3,2},{4,3},{5,4},{6,5},{7,6},{8,7},{9,8},{10,9},{11,1... | collective-permute-start | bytes 36872 | tf_op jit(solution)/shard_map/ppermute | solution.py:227
  8.9 0.0 copy-start
  9.0 1.4 %copy-done = f32[8,3,8,2048]{3,2,1,0:T(8,128)S(1)} copy-done((f32[8,3,8,2048]{3,2,1,0:T(8,128)S(1)}, f32[8,3,8,2048]{3,2,1,0:T(8,128)}, u32[]{:S(2)}) %copy-start) | copy-done | bytes 1572888
  10.4 0.7 %shard_map.37 = (f32[3,4,8,2048]{3,2,1,0:T(8,128)S(1)}, f32[3,4,8,2048]{3,2,1,0:T(8,128)S(1)}) custom-call(f32[8,3,8,2048]{3,2,1,0:T(8,128)S(1)} %copy-done), custom_call_target="tpu_custom_call" | custom-call | tf_op jit(solution)/shard_map/pallas_call | solution.py:48
  11.0 0.0 collective-permute-done.1
  11.0 0.0 collective-permute-done.2
  11.1 14.5 %collective-permute-start.4 = (f32[22,8,128]{2,1,0:T(8,128)S(1)}, f32[22,8,128]{2,1,0:T(8,128)S(1)}, u32[]{:S(2)}, u32[]{:S(2)}) collective-permute-start(f32[22,8,128]{2,1,0:T(8,128)S(1)} %pad_maximum_fusion.1), channel_id=1, source_target_pairs={{0,64},{64,0},{1,65},{65,1},{2,66},{66,2},{3,67},{67,3},{4,68},{68... | collective-permute-start | bytes 270344 | tf_op jit(solution)/shard_map/ppermute | solution.py:230
  25.6 1.9 %collective-permute-start = (f32[3,4,8,2048]{3,2,1,0:T(8,128)S(1)}, f32[3,4,8,2048]{3,2,1,0:T(8,128)S(1)}, u32[]{:S(2)}, u32[]{:S(2)}) collective-permute-start(f32[3,4,8,2048]{3,2,1,0:T(8,128)S(1)} %get-tuple-element.19.high_ref), channel_id=1, source_target_pairs={{0,1},{1,2},{2,3},{3,4},{4,5},{5,6},{6,7},{7,8},{8,9},{9,10},{10,1... | collective-permute-start | bytes 2359304 | tf_op jit(solution)/shard_map/ppermute | solution.py:216
  27.5 5.5 %collective-permute-start.3 = (f32[3,4,8,2048]{3,2,1,0:T(8,128)S(1)}, f32[3,4,8,2048]{3,2,1,0:T(8,128)}, u32[]{:S(2)}, u32[]{:S(2)}) collective-permute-start(f32[3,4,8,2048]{3,2,1,0:T(8,128)S(1)} %get-tuple-element.18.low_ref), channel_id=1, source_target_pairs={{1,0},{2,1},{3,2},{4,3},{5,4},{6,5},{7,6},{8,7},{9,8},{10,9},{11,1... | collective-permute-start | bytes 2359304 | tf_op jit(solution)/shard_map/ppermute | solution.py:217
  33.0 0.0 collective-permute-done.4
  33.1 12.1 %all-gather = f32[8,22,8,128]{3,2,1,0:T(8,128)S(1)} all-gather(f32[2,22,8,128]{3,2,1,0:T(8,128)S(1)} %pad_maximum_fusion), channel_id=2, replica_groups=mesh['x'=4,'zh'=2,'core'=2,'lat'=32] {'x'}, dimensions={0}, use_global_device_ids=true | all-gather | bytes 901120 | tf_op jit(solution)/shard_map/all_gather | solution.py:231
  45.2 5.9 %collective-permute-start.5 = (f32[4,2,22,8,128]{4,3,2,1,0:T(8,128)S(1)}, f32[4,2,22,8,128]{4,3,2,1,0:T(8,128)}, u32[]{:S(2)}, u32[]{:S(2)}) collective-permute-start(f32[4,2,22,8,128]{4,3,2,1,0:T(8,128)S(1)} %bitcast.6), channel_id=1, source_target_pairs={{0,32},{32,0},{1,33},{33,1},{2,34},{34,2},{3,35},{35,3},{4,36},{36... | collective-permute-start | bytes 2162696 | tf_op jit(solution)/shard_map/ppermute | solution.py:232
  51.0 0.1 pad_add_fusion.place_ref
  51.1 1.4 %collective-permute-done.below_ref = f32[3,4,8,2048]{3,2,1,0:T(8,128)S(1)} collective-permute-done((f32[3,4,8,2048]{3,2,1,0:T(8,128)S(1)}, f32[3,4,8,2048]{3,2,1,0:T(8,128)S(1)}, u32[]{:S(2)}, u32[]{:S(2)}) %collective-permute-start) | collective-permute-done | bytes 786464 | tf_op jit(solution)/shard_map/ppermute | solution.py:216
  52.5 0.0 collective-permute-done.3.above_ref
  52.5 1.3 %shard_map.39.band_ref = f32[3,16,8,2048]{3,2,1,0:T(8,128)S(1)} custom-call(f32[3,4,8,2048]{3,2,1,0:T(8,128)S(1)} %collective-permute-done.below_ref, f32[3,4,8,2048]{3,2,1,0:T(8,128)S(1)} %get-tuple-element.18.low_ref, f32[3,4,8,2048]{3,2,1,0:T(8,128)S(1)} %get-tuple-element.19.high_ref, f32[3,4,8,2048]{3,2,1,0:T(8,128)} %collective-permute-done.3.above_ref), custom_call_target="tpu_custom_call" | custom-call | tf_op jit(solution)/shard_map/pallas_call | solution.py:238
  53.8 0.0 collective-permute-done.5.other_ref
  53.8 8.9 %shard_map.40 = f32[8,3,8,2048]{3,2,1,0:T(8,128)} custom-call(s32[4]{0:T(128)S(1)} %pad_add_fusion.place_ref, f32[3,16,8,2048]{3,2,1,0:T(8,128)S(1)} %shard_map.39.band_ref, f32[4,2,22,8,128]{4,3,2,1,0:T(8,128)S(1)} %bitcast.7, f32[4,2,22,8,128]{4,3,2,1,0:T(8,128)} %collective-permute-done.5.other_ref), custom_call_target="tpu_custom_call" | custom-call | tf_op jit(solution)/shard_map/pallas_call | solution.py:245
  (3 shorter events, 0.0 us)
Async XLA Ops:
  0.0 0.8 %copy-start.1 = (f32[4,3,8,128]{3,2,1,0:T(8,128)S(1)}, f32[4,3,8,128]{3,2,1,0:T(8,128)}, u32[]{:S(2)}) copy-start(f32[4,3,8,128]{3,2,1,0:T(8,128)} %wind_ref.1) | copy-start | bytes 147460
  0.8 0.7 %copy-start.2 = (f32[4,8,128]{2,1,0:T(8,128)S(1)}, f32[4,8,128]{2,1,0:T(8,128)}, u32[]{:S(2)}) copy-start(f32[4,8,128]{2,1,0:T(8,128)} %depth_ref.1) | copy-start | bytes 49156
  1.5 9.5 %collective-permute-start.1 = (f32[3,8,128]{2,1,0:T(8,128)S(1)}, f32[3,8,128]{2,1,0:T(8,128)S(1)}, u32[]{:S(2)}, u32[]{:S(2)}) collective-permute-start(f32[3,8,128]{2,1,0:T(8,128)S(1)} %get-tuple-element.15), channel_id=1, source_target_pairs={{0,1},{1,2},{2,3},{3,4},{4,5},{5,6},{6,7},{7,8},{8,9},{9,10},{10,1... | collective-permute-start | bytes 36872 | tf_op jit(solution)/shard_map/ppermute | solution.py:227
  4.8 6.3 %collective-permute-start.2 = (f32[3,8,128]{2,1,0:T(8,128)S(1)}, f32[3,8,128]{2,1,0:T(8,128)S(1)}, u32[]{:S(2)}, u32[]{:S(2)}) collective-permute-start(f32[3,8,128]{2,1,0:T(8,128)S(1)} %get-tuple-element.16), channel_id=1, source_target_pairs={{1,0},{2,1},{3,2},{4,3},{5,4},{6,5},{7,6},{8,7},{9,8},{10,9},{11,1... | collective-permute-start | bytes 36872 | tf_op jit(solution)/shard_map/ppermute | solution.py:227
  8.9 1.4 %copy-start = (f32[8,3,8,2048]{3,2,1,0:T(8,128)S(1)}, f32[8,3,8,2048]{3,2,1,0:T(8,128)}, u32[]{:S(2)}) copy-start(f32[8,3,8,2048]{3,2,1,0:T(8,128)} %state_ref.1) | copy-start | bytes 4718596
  11.1 22.0 %collective-permute-start.4 = (f32[22,8,128]{2,1,0:T(8,128)S(1)}, f32[22,8,128]{2,1,0:T(8,128)S(1)}, u32[]{:S(2)}, u32[]{:S(2)}) collective-permute-start(f32[22,8,128]{2,1,0:T(8,128)S(1)} %pad_maximum_fusion.1), channel_id=1, source_target_pairs={{0,64},{64,0},{1,65},{65,1},{2,66},{66,2},{3,67},{67,3},{4,68},{68... | collective-permute-start | bytes 270344 | tf_op jit(solution)/shard_map/ppermute | solution.py:230
  25.6 26.9 %collective-permute-start = (f32[3,4,8,2048]{3,2,1,0:T(8,128)S(1)}, f32[3,4,8,2048]{3,2,1,0:T(8,128)S(1)}, u32[]{:S(2)}, u32[]{:S(2)}) collective-permute-start(f32[3,4,8,2048]{3,2,1,0:T(8,128)S(1)} %get-tuple-element.19.high_ref), channel_id=1, source_target_pairs={{0,1},{1,2},{2,3},{3,4},{4,5},{5,6},{6,7},{7,8},{8,9},{9,10},{10,1... | collective-permute-start | bytes 2359304 | tf_op jit(solution)/shard_map/ppermute | solution.py:216
  27.5 24.9 %collective-permute-start.3 = (f32[3,4,8,2048]{3,2,1,0:T(8,128)S(1)}, f32[3,4,8,2048]{3,2,1,0:T(8,128)}, u32[]{:S(2)}, u32[]{:S(2)}) collective-permute-start(f32[3,4,8,2048]{3,2,1,0:T(8,128)S(1)} %get-tuple-element.18.low_ref), channel_id=1, source_target_pairs={{1,0},{2,1},{3,2},{4,3},{5,4},{6,5},{7,6},{8,7},{9,8},{10,9},{11,1... | collective-permute-start | bytes 2359304 | tf_op jit(solution)/shard_map/ppermute | solution.py:217
  45.2 8.7 %collective-permute-start.5 = (f32[4,2,22,8,128]{4,3,2,1,0:T(8,128)S(1)}, f32[4,2,22,8,128]{4,3,2,1,0:T(8,128)}, u32[]{:S(2)}, u32[]{:S(2)}) collective-permute-start(f32[4,2,22,8,128]{4,3,2,1,0:T(8,128)S(1)} %bitcast.6), channel_id=1, source_target_pairs={{0,32},{32,0},{1,33},{33,1},{2,34},{34,2},{3,35},{35,3},{4,36},{36... | collective-permute-start | bytes 2162696 | tf_op jit(solution)/shard_map/ppermute | solution.py:232

commit v4 on v3

--- a/solution.py
+++ b/solution.py
@@ -7,7 +7,7 @@
 
 STEPS = 4
 HALO = 4
-UNROLL = 2
+BLOCK = 4
 LANES = 128
 
 time_step = 0.2
@@ -19,6 +19,7 @@
 HEIGHT = 2.0 * KEEP / time_step
 
 VMEM = pl.BlockSpec(memory_space=pltpu.VMEM)
+HBM = pl.BlockSpec(memory_space=pl.ANY)
 SMEM = pl.BlockSpec(memory_space=pltpu.SMEM)
 
 
@@ -72,7 +73,7 @@
                 out[2, 4:] = block[near, :4]
 
 
-def step_row(source, target, plus, minus, raw, moment, row, crow, tiles, edge):
+def step_row(source, target, plus, minus, moment, row, tiles, edge):
     def at(field, r, tile):
         return source[field, r, :, pl.ds(tile * LANES, LANES)]
 
@@ -91,7 +92,7 @@
         return held[field, tile]
 
     def coefficient(ref, tile, channel):
-        line = ref[tile, crow, pl.ds(moment * 4 + channel, 1), :]
+        line = ref[tile, row - 1, pl.ds(moment * 4 + channel, 1), :]
         return jnp.broadcast_to(line, (8, LANES))
 
     for tile in range(tiles):
@@ -107,8 +108,8 @@
         to_west = coefficient(minus, tile, 0)
         to_north = coefficient(plus, tile, 1)
         to_south = coefficient(minus, tile, 1)
-        turn = coefficient(raw, tile, 2)
-        depth = coefficient(raw, tile, 3)
+        turn = coefficient(plus, tile, 2)
+        depth = coefficient(plus, tile, 3)
         new = [
             (middle[f] + to_east * east[f])
             + (to_west * west[f] + to_north * north[f])
@@ -122,31 +123,36 @@
             target(field, row, tile, new[field])
 
 
-def lay_band(below_ref, low_ref, high_ref, above_ref, band_ref):
-    for field in range(band_ref.shape[0]):
-        start = 0
-        for ref in (below_ref, low_ref, high_ref, above_ref):
-            for row in range(ref.shape[1]):
-                band_ref[field, start + row] = ref[field, row]
-            start += ref.shape[1]
-
-
 def advance_all(
-    place_ref, band_ref, mine_ref, other_ref, out_ref, first, second, last, raw, plus, minus, sems
+    place_ref, below_ref, low_ref, high_ref, above_ref, mine_ref, other_hbm, out_ref,
+    first, second, plus, minus, other_ref, laid, sem, left
 ):
-    tiles = raw.shape[0]
+    tiles = plus.shape[0]
     rows = out_ref.shape[2]
-
-    @pl.loop(0, tiles // 4)
-    def _(quad):
-        for core, gathered in enumerate((mine_ref, other_ref)):
+    half = low_ref.shape[1]
+    copies = [
+        pltpu.make_async_copy(below_ref, first.at[:, pl.ds(0, HALO)], laid.at[0]),
+        pltpu.make_async_copy(above_ref, first.at[:, pl.ds(HALO + rows, HALO)], laid.at[1]),
+    ]
+    fetches = [
+        pltpu.make_async_copy(other_hbm.at[quad, side], other_ref.at[quad, side], sem.at[quad, side])
+        for quad in range(tiles // 4)
+        for side in range(2)
+    ]
+    for each in fetches + copies:
+        each.start()
+    channel = lax.broadcasted_iota(jnp.int32, (8, LANES), 0) % 4
+    spread = jnp.where(channel < 2, jnp.float32(SPREAD), jnp.float32(0.0))
+
+    def lay(core, gathered):
+        @pl.loop(0, tiles // 4)
+        def _(quad):
             for side in range(2):
                 tile = quad * 4 + (side ^ place_ref[2]) * 2 + (core ^ place_ref[3])
 
                 def put(row, line, value):
                     lines = pl.ds(line, value.shape[0])
-                    raw[tile, row, lines, :] = value
-                    plus[tile, row, lines, :] = SPREAD + value
+                    plus[tile, row, lines, :] = value + spread[: value.shape[0]]
                     minus[tile, row, lines, :] = SPREAD - value
 
                 for row in range(rows):
@@ -158,46 +164,58 @@
                     put(far, 0, gathered[quad, side, start + 2, :4])
                     put(near, 8, gathered[quad, side, start + 2, 4:])
 
+    lay(0, mine_ref)
+    for start, ref in ((HALO, low_ref), (HALO + half, high_ref)):
+
+        @pl.loop(0, half)
+        def _(row):
+            for field in range(3):
+                first[field, start + row] = ref[field, row]
+
+    for each in fetches:
+        each.wait()
+    lay(1, other_ref)
+
+    for each in copies:
+        each.wait()
     lane = lax.broadcasted_iota(jnp.int32, (8, LANES), 1)
     edge = (lane == 0, lane == LANES - 1)
 
     def leaving(field, row):
-        return pltpu.make_async_copy(last.at[field, row], out_ref.at[:, field, row], sems.at[field, row])
-
-    for moment, (source, goal) in enumerate([(band_ref, first), (first, second), (second, first), (first, last)]):
-        final = moment == STEPS - 1
-
-        def rows_of(start, count):
+        return pltpu.make_async_copy(first.at[field, HALO + row], out_ref.at[:, field, row], left.at[field, row])
+
+    @pl.loop(0, STEPS // 2)
+    def _(turn):
+        for half, (source, goal) in enumerate([(first, second), (second, first)]):
+            moment = 2 * turn + half
+            begin, end = (moment + 1, rows + 2 * HALO - 1 - moment)
+            final = jnp.logical_and(turn == STEPS // 2 - 1, half == 1)
+            scales = [jnp.where(final, KEEP**STEPS * (HEIGHT if field == 0 else 1.0), 1.0) for field in range(3)]
+
             def target(field, row, tile, value):
-                lanes = pl.ds(tile * LANES, LANES)
-                if final:
-                    scale = KEEP**STEPS * (HEIGHT if field == 0 else 1.0)
-                    goal[field, row - HALO, :, lanes] = value * scale
-                else:
-                    goal[field, row, :, lanes] = value
-
-            for row in range(count):
-                row += start
-                step_row(source, target, plus, minus, raw, moment, row, row - 1, tiles, edge)
-                if final:
-                    for field in range(3):
-                        leaving(field, row - HALO).start()
-
-        begin, count = (moment + 1, rows + 2 * (STEPS - 1 - moment))
-
-        @pl.loop(begin, begin + count, step=UNROLL)
-        def _(row):
-            rows_of(row, UNROLL)
-
-        if not final:
-
-            @pl.when(place_ref[0] == 0)
-            def _():
-                goal[:, HALO - 1] = jnp.zeros_like(goal[:, HALO - 1])
-
-            @pl.when(place_ref[0] == place_ref[1] - 1)
-            def _():
-                goal[:, HALO + rows] = jnp.zeros_like(goal[:, HALO + rows])
+                if half:
+                    value = value * scales[field]
+                goal[field, row, :, pl.ds(tile * LANES, LANES)] = value
+
+            @pl.loop(0, (end - begin + BLOCK - 1) // BLOCK)
+            def _(block):
+                start = jnp.minimum(begin + block * BLOCK, end - BLOCK)
+                for row in range(BLOCK):
+                    row += start
+                    step_row(source, target, plus, minus, moment, row, tiles, edge)
+                if half:
+
+                    @pl.when(final)
+                    def _():
+                        for row in range(BLOCK):
+                            for field in range(3):
+                                leaving(field, start + row - HALO).start()
+
+            for grid_edge, row in ((0, HALO - 1), (place_ref[1] - 1, HALO + rows)):
+
+                @pl.when(place_ref[0] == grid_edge)
+                def _():
+                    goal[:, row] = jnp.zeros_like(goal[:, row])
 
     @pl.loop(0, rows)
     def _(row):
@@ -234,30 +252,23 @@
     place = [lax.axis_index("lat"), count, lax.axis_index("zh"), lax.axis_index("core")]
     place = jnp.stack([jnp.int32(number) for number in place])
     table = pltpu.VMEM((tiles, rows + 6, STEPS * 4, LANES), jnp.float32)
-    band = (fields, rows + 2 * HALO, vectors, lon)
-    laid = pl.pallas_call(
-        lay_band,
-        out_shape=jax.ShapeDtypeStruct(band, jnp.float32),
-        in_specs=[VMEM] * 4,
-        out_specs=VMEM,
-        compiler_params=room(8),
-    )(below, low, high, above)
     return pl.pallas_call(
         advance_all,
         out_shape=jax.ShapeDtypeStruct(perturbation.shape, perturbation.dtype),
-        in_specs=[SMEM] + [VMEM] * 3,
-        out_specs=pl.BlockSpec(memory_space=pl.ANY),
+        in_specs=[SMEM, HBM, VMEM, VMEM, HBM, VMEM, HBM],
+        out_specs=HBM,
         scratch_shapes=[
-            pltpu.VMEM(band, jnp.float32),
-            pltpu.VMEM(band, jnp.float32),
-            pltpu.VMEM((fields, rows, vectors, lon), jnp.float32),
+            pltpu.VMEM((fields, rows + 2 * HALO, vectors, lon), jnp.float32),
+            pltpu.VMEM((fields, rows + 2 * HALO, vectors, lon), jnp.float32),
             table,
             table,
-            table,
+            pltpu.VMEM(other.shape, jnp.float32),
+            pltpu.SemaphoreType.DMA((2,)),
+            pltpu.SemaphoreType.DMA((tiles // 4, 2)),
             pltpu.SemaphoreType.DMA((fields, rows)),
         ],
         compiler_params=room(14),
-    )(place, laid, mine, other)
+    )(place, below, low, high, above, mine, other)
 
 
 def solution(mesh):

time: 63.6 us -> 63 us (level)
    pallas_call x1 -> x0, Pallas kernels: 1.34 us -> none  [shards(): pl.pallas_call(lay_band, out_shape=jax.ShapeDtypeStruct(band, jnp.float32...]
    pallas_call x1, Pallas kernels: 8.9 us -> 9.62 us  [shards(): pl.pallas_call(advance_all, out_shape=jax.ShapeDtypeStruct(perturbation.s...]
  transfers between devices with their start and end apart: 6 -> 6, of which waited for: 1 -> 2; matrix products, arithmetic and copies ran while one was open for 0% -> 0% of each run, Pallas kernels for 3% -> 1%
where the time goes in v4:
time: 63 us; the launch traced here: 62.6 us
  starting transfers between devices  35.2 us (56%)
  blocking collectives  12.1 us (19%)
  Pallas kernels  10.3 us (16%)
  local copies, waits for them, and re-layouts  2.92 us (5%)
  waiting for transfers between devices  1.85 us (3%)
    ppermute x1, starting transfers between devices, shards(): mine = jnp.stack([own, lax.ppermute(own, 'zh', swap)])  14.5 us
    all_gather x1, blocking collectives, shards(): mine = lax.all_gather(mine, 'x', axis=0)  12.1 us
    pallas_call x1, Pallas kernels, shards(): pl.pallas_call(advance_all, out_shape=jax.ShapeDtypeStruct(perturbation.s...  9.62 us
    ppermute x1, starting transfers between devices, shards(): other = lax.ppermute(mine, 'core', swap)  5.87 us
    ppermute x1, starting transfers between devices, shards(): above = lax.ppermute(low, 'lat', down)  5.47 us
    ppermute x1, starting transfers between devices, shards(): lax.ppermute(to_down, 'lat', down)  4.19 us
    ppermute x1, starting transfers between devices, shards(): lax.ppermute(to_up, 'lat', up)  3.2 us
    unnamed x6, local copies, waits for them, and re-layouts  2.92 us
  transfers between devices with their start and end apart: 6, of which 2 were waited for; matrix products, arithmetic and copies ran while one was open for 0% of the time, Pallas kernels for 1%

profile of v4, /device:TPU:33, one launch (start us, length us, event | category | flops | bytes accessed | tf_op | source)
XLA Modules:
  0.0 62.6 jit_solution(5354567343058537066)
XLA Ops:
  0.0 0.0 copy-start.1
  0.0 0.8 %copy-done.1 = f32[4,3,8,128]{3,2,1,0:T(8,128)S(1)} copy-done((f32[4,3,8,128]{3,2,1,0:T(8,128)S(1)}, f32[4,3,8,128]{3,2,1,0:T(8,128)}, u32[]{:S(2)}) %copy-start.1) | copy-done | bytes 49176
  0.8 0.0 copy-start.2
  0.8 0.7 %copy-done.2 = f32[4,8,128]{2,1,0:T(8,128)S(1)} copy-done((f32[4,8,128]{2,1,0:T(8,128)S(1)}, f32[4,8,128]{2,1,0:T(8,128)}, u32[]{:S(2)}) %copy-start.2) | copy-done | bytes 16408
  1.5 3.2 %collective-permute-start.1 = (f32[3,8,128]{2,1,0:T(8,128)S(1)}, f32[3,8,128]{2,1,0:T(8,128)S(1)}, u32[]{:S(2)}, u32[]{:S(2)}) collective-permute-start(f32[3,8,128]{2,1,0:T(8,128)S(1)} %get-tuple-element.15), channel_id=1, source_target_pairs={{0,1},{1,2},{2,3},{3,4},{4,5},{5,6},{6,7},{7,8},{8,9},{9,10},{10,1... | collective-permute-start | bytes 36872 | tf_op jit(solution)/shard_map/ppermute | solution.py:245
  4.8 4.2 %collective-permute-start.2 = (f32[3,8,128]{2,1,0:T(8,128)S(1)}, f32[3,8,128]{2,1,0:T(8,128)S(1)}, u32[]{:S(2)}, u32[]{:S(2)}) collective-permute-start(f32[3,8,128]{2,1,0:T(8,128)S(1)} %get-tuple-element.16), channel_id=1, source_target_pairs={{1,0},{2,1},{3,2},{4,3},{5,4},{6,5},{7,6},{8,7},{9,8},{10,9},{11,1... | collective-permute-start | bytes 36872 | tf_op jit(solution)/shard_map/ppermute | solution.py:245
  8.9 0.0 copy-start
  9.0 1.4 %copy-done = f32[8,3,8,2048]{3,2,1,0:T(8,128)S(1)} copy-done((f32[8,3,8,2048]{3,2,1,0:T(8,128)S(1)}, f32[8,3,8,2048]{3,2,1,0:T(8,128)}, u32[]{:S(2)}) %copy-start) | copy-done | bytes 1572888
  10.4 0.7 %shard_map.37 = (f32[3,4,8,2048]{3,2,1,0:T(8,128)S(1)}, f32[3,4,8,2048]{3,2,1,0:T(8,128)S(1)}) custom-call(f32[8,3,8,2048]{3,2,1,0:T(8,128)S(1)} %copy-done), custom_call_target="tpu_custom_call" | custom-call | tf_op jit(solution)/shard_map/pallas_call | solution.py:49
  11.0 0.0 collective-permute-done.1
  11.0 0.0 collective-permute-done.2
  11.1 14.5 %collective-permute-start.4 = (f32[22,8,128]{2,1,0:T(8,128)S(1)}, f32[22,8,128]{2,1,0:T(8,128)S(1)}, u32[]{:S(2)}, u32[]{:S(2)}) collective-permute-start(f32[22,8,128]{2,1,0:T(8,128)S(1)} %pad_maximum_fusion.1), channel_id=1, source_target_pairs={{0,64},{64,0},{1,65},{65,1},{2,66},{66,2},{3,67},{67,3},{4,68},{68... | collective-permute-start | bytes 270344 | tf_op jit(solution)/shard_map/ppermute | solution.py:248
  25.6 1.9 %collective-permute-start = (f32[3,4,8,2048]{3,2,1,0:T(8,128)S(1)}, f32[3,4,8,2048]{3,2,1,0:T(8,128)S(1)}, u32[]{:S(2)}, u32[]{:S(2)}) collective-permute-start(f32[3,4,8,2048]{3,2,1,0:T(8,128)S(1)} %get-tuple-element.19.high_ref), channel_id=1, source_target_pairs={{0,1},{1,2},{2,3},{3,4},{4,5},{5,6},{6,7},{7,8},{8,9},{9,10},{10,1... | collective-permute-start | bytes 2359304 | tf_op jit(solution)/shard_map/ppermute | solution.py:234
  27.5 5.5 %collective-permute-start.3 = (f32[3,4,8,2048]{3,2,1,0:T(8,128)S(1)}, f32[3,4,8,2048]{3,2,1,0:T(8,128)}, u32[]{:S(2)}, u32[]{:S(2)}) collective-permute-start(f32[3,4,8,2048]{3,2,1,0:T(8,128)S(1)} %get-tuple-element.18.low_ref), channel_id=1, source_target_pairs={{1,0},{2,1},{3,2},{4,3},{5,4},{6,5},{7,6},{8,7},{9,8},{10,9},{11,1... | collective-permute-start | bytes 2359304 | tf_op jit(solution)/shard_map/ppermute | solution.py:235
  33.0 0.0 collective-permute-done.4
  33.1 12.1 %all-gather = f32[8,22,8,128]{3,2,1,0:T(8,128)S(1)} all-gather(f32[2,22,8,128]{3,2,1,0:T(8,128)S(1)} %pad_maximum_fusion), channel_id=2, replica_groups=mesh['x'=4,'zh'=2,'core'=2,'lat'=32] {'x'}, dimensions={0}, use_global_device_ids=true | all-gather | bytes 901120 | tf_op jit(solution)/shard_map/all_gather | solution.py:249
  45.2 5.9 %collective-permute-start.5 = (f32[4,2,22,8,128]{4,3,2,1,0:T(8,128)S(1)}, f32[4,2,22,8,128]{4,3,2,1,0:T(8,128)}, u32[]{:S(2)}, u32[]{:S(2)}) collective-permute-start(f32[4,2,22,8,128]{4,3,2,1,0:T(8,128)S(1)} %bitcast.6), channel_id=1, source_target_pairs={{0,32},{32,0},{1,33},{33,1},{2,34},{34,2},{3,35},{35,3},{4,36},{36... | collective-permute-start | bytes 2162696 | tf_op jit(solution)/shard_map/ppermute | solution.py:250
  51.0 0.1 pad_add_fusion.place_ref
  51.1 1.4 %collective-permute-done.below_ref = f32[3,4,8,2048]{3,2,1,0:T(8,128)S(1)} collective-permute-done((f32[3,4,8,2048]{3,2,1,0:T(8,128)S(1)}, f32[3,4,8,2048]{3,2,1,0:T(8,128)S(1)}, u32[]{:S(2)}, u32[]{:S(2)}) %collective-permute-start) | collective-permute-done | bytes 786464 | tf_op jit(solution)/shard_map/ppermute | solution.py:234
  52.5 0.0 collective-permute-done.3.above_ref
  52.5 0.5 collective-permute-done.5.other_hbm
  53.0 9.6 %shard_map.39 = f32[8,3,8,2048]{3,2,1,0:T(8,128)} custom-call(s32[4]{0:T(128)S(1)} %pad_add_fusion.place_ref, f32[3,4,8,2048]{3,2,1,0:T(8,128)S(1)} %collective-permute-done.below_ref, f32[3,4,8,2048]{3,2,1,0:T(8,128)S(1)} %get-tuple-element.18.low_ref, f32[3,4,8,2048]{3,2,1,0:T(8,128)S(1)} %get-tuple-element.19.high_ref, ...), custom_call_target="tpu_custom_call" | custom-call | tf_op jit(solution)/shard_map/pallas_call | solution.py:255
  (3 shorter events, 0.0 us)
Async XLA Ops:
  0.0 0.8 %copy-start.1 = (f32[4,3,8,128]{3,2,1,0:T(8,128)S(1)}, f32[4,3,8,128]{3,2,1,0:T(8,128)}, u32[]{:S(2)}) copy-start(f32[4,3,8,128]{3,2,1,0:T(8,128)} %wind_ref.1) | copy-start | bytes 147460
  0.8 0.7 %copy-start.2 = (f32[4,8,128]{2,1,0:T(8,128)S(1)}, f32[4,8,128]{2,1,0:T(8,128)}, u32[]{:S(2)}) copy-start(f32[4,8,128]{2,1,0:T(8,128)} %depth_ref.1) | copy-start | bytes 49156
  1.5 9.5 %collective-permute-start.1 = (f32[3,8,128]{2,1,0:T(8,128)S(1)}, f32[3,8,128]{2,1,0:T(8,128)S(1)}, u32[]{:S(2)}, u32[]{:S(2)}) collective-permute-start(f32[3,8,128]{2,1,0:T(8,128)S(1)} %get-tuple-element.15), channel_id=1, source_target_pairs={{0,1},{1,2},{2,3},{3,4},{4,5},{5,6},{6,7},{7,8},{8,9},{9,10},{10,1... | collective-permute-start | bytes 36872 | tf_op jit(solution)/shard_map/ppermute | solution.py:245
  4.8 6.3 %collective-permute-start.2 = (f32[3,8,128]{2,1,0:T(8,128)S(1)}, f32[3,8,128]{2,1,0:T(8,128)S(1)}, u32[]{:S(2)}, u32[]{:S(2)}) collective-permute-start(f32[3,8,128]{2,1,0:T(8,128)S(1)} %get-tuple-element.16), channel_id=1, source_target_pairs={{1,0},{2,1},{3,2},{4,3},{5,4},{6,5},{7,6},{8,7},{9,8},{10,9},{11,1... | collective-permute-start | bytes 36872 | tf_op jit(solution)/shard_map/ppermute | solution.py:245
  8.9 1.4 %copy-start = (f32[8,3,8,2048]{3,2,1,0:T(8,128)S(1)}, f32[8,3,8,2048]{3,2,1,0:T(8,128)}, u32[]{:S(2)}) copy-start(f32[8,3,8,2048]{3,2,1,0:T(8,128)} %state_ref.1) | copy-start | bytes 4718596
  11.1 22.0 %collective-permute-start.4 = (f32[22,8,128]{2,1,0:T(8,128)S(1)}, f32[22,8,128]{2,1,0:T(8,128)S(1)}, u32[]{:S(2)}, u32[]{:S(2)}) collective-permute-start(f32[22,8,128]{2,1,0:T(8,128)S(1)} %pad_maximum_fusion.1), channel_id=1, source_target_pairs={{0,64},{64,0},{1,65},{65,1},{2,66},{66,2},{3,67},{67,3},{4,68},{68... | collective-permute-start | bytes 270344 | tf_op jit(solution)/shard_map/ppermute | solution.py:248
  25.6 26.9 %collective-permute-start = (f32[3,4,8,2048]{3,2,1,0:T(8,128)S(1)}, f32[3,4,8,2048]{3,2,1,0:T(8,128)S(1)}, u32[]{:S(2)}, u32[]{:S(2)}) collective-permute-start(f32[3,4,8,2048]{3,2,1,0:T(8,128)S(1)} %get-tuple-element.19.high_ref), channel_id=1, source_target_pairs={{0,1},{1,2},{2,3},{3,4},{4,5},{5,6},{6,7},{7,8},{8,9},{9,10},{10,1... | collective-permute-start | bytes 2359304 | tf_op jit(solution)/shard_map/ppermute | solution.py:234
  27.5 24.9 %collective-permute-start.3 = (f32[3,4,8,2048]{3,2,1,0:T(8,128)S(1)}, f32[3,4,8,2048]{3,2,1,0:T(8,128)}, u32[]{:S(2)}, u32[]{:S(2)}) collective-permute-start(f32[3,4,8,2048]{3,2,1,0:T(8,128)S(1)} %get-tuple-element.18.low_ref), channel_id=1, source_target_pairs={{1,0},{2,1},{3,2},{4,3},{5,4},{6,5},{7,6},{8,7},{9,8},{10,9},{11,1... | collective-permute-start | bytes 2359304 | tf_op jit(solution)/shard_map/ppermute | solution.py:235
  45.2 7.8 %collective-permute-start.5 = (f32[4,2,22,8,128]{4,3,2,1,0:T(8,128)S(1)}, f32[4,2,22,8,128]{4,3,2,1,0:T(8,128)}, u32[]{:S(2)}, u32[]{:S(2)}) collective-permute-start(f32[4,2,22,8,128]{4,3,2,1,0:T(8,128)S(1)} %bitcast.6), channel_id=1, source_target_pairs={{0,32},{32,0},{1,33},{33,1},{2,34},{34,2},{3,35},{35,3},{4,36},{36... | collective-permute-start | bytes 2162696 | tf_op jit(solution)/shard_map/ppermute | solution.py:250

commit v5 on v4

--- a/solution.py
+++ b/solution.py
@@ -55,7 +55,15 @@
     )(state)
 
 
-def pack(wind_ref, depth_ref, own_ref, up_ref, down_ref):
+def pack(wind_hbm, depth_hbm, own_ref, up_ref, down_ref, wind_ref, depth_ref, sems):
+    copies = [
+        pltpu.make_async_copy(wind_hbm, wind_ref, sems.at[0]),
+        pltpu.make_async_copy(depth_hbm, depth_ref, sems.at[1]),
+    ]
+    for copy in copies:
+        copy.start()
+    for copy in copies:
+        copy.wait()
     for pair in range(STEPS // 2):
         planes = []
         for moment in (2 * pair, 2 * pair + 1):
@@ -238,10 +246,15 @@
     own, to_up, to_down = pl.pallas_call(
         pack,
         out_shape=(jax.ShapeDtypeStruct((2 * rows, 8, LANES), jnp.float32), few, few),
-        in_specs=[VMEM] * 2,
+        in_specs=[pl.BlockSpec(memory_space=pltpu.HBM)] * 2,
         out_specs=(VMEM,) * 3,
-        compiler_params=room(4),
-    )(wind_coriolis, depth_field)
+        scratch_shapes=[
+            pltpu.VMEM(wind_coriolis.shape, jnp.float32),
+            pltpu.VMEM(depth_field.shape, jnp.float32),
+            pltpu.SemaphoreType.DMA((2,)),
+        ],
+        compiler_params=room(2),
+    )(*(pltpu.with_memory_space_constraint(part, pltpu.HBM) for part in (wind_coriolis, depth_field)))
     own = jnp.concatenate([own, lax.ppermute(to_up, "lat", up), lax.ppermute(to_down, "lat", down)])
     own, low, high = lax.optimization_barrier((own, low, high))
     swap = [(0, 1), (1, 0)]

time: 63 us -> 62.2 us (0.987)
  local copies, waits for them, and re-layouts: 2.92 us -> 1.4 us
  Pallas kernels: 10.3 us -> 11.1 us
    unnamed x6 -> x2, local copies, waits for them, and re-layouts: 2.92 us -> 1.4 us
    pallas_call x1, Pallas kernels: 0.02 us -> 0.83 us  [shards(): pl.pallas_call(pack, out_shape=(jax.ShapeDtypeStruct((2 * rows, 8, LANES)...]
where the time goes in v5:
time: 62.2 us; the launch traced here: 61.9 us
  starting transfers between devices  35.2 us (57%)
  blocking collectives  12.1 us (19%)
  Pallas kernels  11.1 us (18%)
  waiting for transfers between devices  1.85 us (3%)
  local copies, waits for them, and re-layouts  1.4 us (2%)
    ppermute x1, starting transfers between devices, shards(): mine = jnp.stack([own, lax.ppermute(own, 'zh', swap)])  14.5 us
    all_gather x1, blocking collectives, shards(): mine = lax.all_gather(mine, 'x', axis=0)  12.1 us
    pallas_call x1, Pallas kernels, shards(): pl.pallas_call(advance_all, out_shape=jax.ShapeDtypeStruct(perturbation.s...  9.62 us
    ppermute x1, starting transfers between devices, shards(): other = lax.ppermute(mine, 'core', swap)  5.87 us
    ppermute x1, starting transfers between devices, shards(): above = lax.ppermute(low, 'lat', down)  5.47 us
    ppermute x1, starting transfers between devices, shards(): lax.ppermute(to_down, 'lat', down)  4.19 us
    ppermute x1, starting transfers between devices, shards(): lax.ppermute(to_up, 'lat', up)  3.2 us
    ppermute x1, starting transfers between devices, shards(): below = lax.ppermute(high, 'lat', up)  1.92 us
  transfers between devices with their start and end apart: 6, of which 2 were waited for; matrix products, arithmetic and copies ran while one was open for 0% of the time, Pallas kernels for 1%

profile of v5, /device:TPU:33, one launch (start us, length us, event | category | flops | bytes accessed | tf_op | source)
XLA Modules:
  0.0 61.9 jit_solution(5123846429480715342)
XLA Ops:
  0.0 0.8 %shard_map.38 = (f32[16,8,128]{2,1,0:T(8,128)S(1)}, f32[3,8,128]{2,1,0:T(8,128)S(1)}, f32[3,8,128]{2,1,0:T(8,128)S(1)}) custom-call(f32[4,3,8,128]{3,2,1,0:T(8,128)} %wind_hbm.1, f32[4,8,128]{2,1,0:T(8,128)} %depth_hbm.1), custom_call_target="tpu_custom_call" | custom-call | tf_op jit(solution)/shard_map/pallas_call | solution.py:246
  0.8 3.2 %collective-permute-start.1 = (f32[3,8,128]{2,1,0:T(8,128)S(1)}, f32[3,8,128]{2,1,0:T(8,128)S(1)}, u32[]{:S(2)}, u32[]{:S(2)}) collective-permute-start(f32[3,8,128]{2,1,0:T(8,128)S(1)} %get-tuple-element.15), channel_id=1, source_target_pairs={{0,1},{1,2},{2,3},{3,4},{4,5},{5,6},{6,7},{7,8},{8,9},{9,10},{10,1... | collective-permute-start | bytes 36872 | tf_op jit(solution)/shard_map/ppermute | solution.py:258
  4.1 4.2 %collective-permute-start.2 = (f32[3,8,128]{2,1,0:T(8,128)S(1)}, f32[3,8,128]{2,1,0:T(8,128)S(1)}, u32[]{:S(2)}, u32[]{:S(2)}) collective-permute-start(f32[3,8,128]{2,1,0:T(8,128)S(1)} %get-tuple-element.16), channel_id=1, source_target_pairs={{1,0},{2,1},{3,2},{4,3},{5,4},{6,5},{7,6},{8,7},{9,8},{10,9},{11,1... | collective-permute-start | bytes 36872 | tf_op jit(solution)/shard_map/ppermute | solution.py:258
  8.3 0.0 copy-start
  8.3 1.4 %copy-done = f32[8,3,8,2048]{3,2,1,0:T(8,128)S(1)} copy-done((f32[8,3,8,2048]{3,2,1,0:T(8,128)S(1)}, f32[8,3,8,2048]{3,2,1,0:T(8,128)}, u32[]{:S(2)}) %copy-start) | copy-done | bytes 1572888
  9.7 0.7 %shard_map.37 = (f32[3,4,8,2048]{3,2,1,0:T(8,128)S(1)}, f32[3,4,8,2048]{3,2,1,0:T(8,128)S(1)}) custom-call(f32[8,3,8,2048]{3,2,1,0:T(8,128)S(1)} %copy-done), custom_call_target="tpu_custom_call" | custom-call | tf_op jit(solution)/shard_map/pallas_call | solution.py:49
  10.3 0.0 collective-permute-done.1
  10.3 0.0 collective-permute-done.2
  10.4 14.5 %collective-permute-start.4 = (f32[22,8,128]{2,1,0:T(8,128)S(1)}, f32[22,8,128]{2,1,0:T(8,128)S(1)}, u32[]{:S(2)}, u32[]{:S(2)}) collective-permute-start(f32[22,8,128]{2,1,0:T(8,128)S(1)} %pad_maximum_fusion.1), channel_id=1, source_target_pairs={{0,64},{64,0},{1,65},{65,1},{2,66},{66,2},{3,67},{67,3},{4,68},{68... | collective-permute-start | bytes 270344 | tf_op jit(solution)/shard_map/ppermute | solution.py:261
  24.9 1.9 %collective-permute-start = (f32[3,4,8,2048]{3,2,1,0:T(8,128)S(1)}, f32[3,4,8,2048]{3,2,1,0:T(8,128)S(1)}, u32[]{:S(2)}, u32[]{:S(2)}) collective-permute-start(f32[3,4,8,2048]{3,2,1,0:T(8,128)S(1)} %get-tuple-element.19.high_ref), channel_id=1, source_target_pairs={{0,1},{1,2},{2,3},{3,4},{4,5},{5,6},{6,7},{7,8},{8,9},{9,10},{10,1... | collective-permute-start | bytes 2359304 | tf_op jit(solution)/shard_map/ppermute | solution.py:242
  26.8 5.5 %collective-permute-start.3 = (f32[3,4,8,2048]{3,2,1,0:T(8,128)S(1)}, f32[3,4,8,2048]{3,2,1,0:T(8,128)}, u32[]{:S(2)}, u32[]{:S(2)}) collective-permute-start(f32[3,4,8,2048]{3,2,1,0:T(8,128)S(1)} %get-tuple-element.18.low_ref), channel_id=1, source_target_pairs={{1,0},{2,1},{3,2},{4,3},{5,4},{6,5},{7,6},{8,7},{9,8},{10,9},{11,1... | collective-permute-start | bytes 2359304 | tf_op jit(solution)/shard_map/ppermute | solution.py:243
  32.3 0.0 collective-permute-done.4
  32.4 12.1 %all-gather = f32[8,22,8,128]{3,2,1,0:T(8,128)S(1)} all-gather(f32[2,22,8,128]{3,2,1,0:T(8,128)S(1)} %pad_maximum_fusion), channel_id=2, replica_groups=mesh['x'=4,'zh'=2,'core'=2,'lat'=32] {'x'}, dimensions={0}, use_global_device_ids=true | all-gather | bytes 901120 | tf_op jit(solution)/shard_map/all_gather | solution.py:262
  44.5 5.9 %collective-permute-start.5 = (f32[4,2,22,8,128]{4,3,2,1,0:T(8,128)S(1)}, f32[4,2,22,8,128]{4,3,2,1,0:T(8,128)}, u32[]{:S(2)}, u32[]{:S(2)}) collective-permute-start(f32[4,2,22,8,128]{4,3,2,1,0:T(8,128)S(1)} %bitcast.6), channel_id=1, source_target_pairs={{0,32},{32,0},{1,33},{33,1},{2,34},{34,2},{3,35},{35,3},{4,36},{36... | collective-permute-start | bytes 2162696 | tf_op jit(solution)/shard_map/ppermute | solution.py:263
  50.3 0.1 pad_add_fusion.place_ref
  50.4 1.4 %collective-permute-done.below_ref = f32[3,4,8,2048]{3,2,1,0:T(8,128)S(1)} collective-permute-done((f32[3,4,8,2048]{3,2,1,0:T(8,128)S(1)}, f32[3,4,8,2048]{3,2,1,0:T(8,128)S(1)}, u32[]{:S(2)}, u32[]{:S(2)}) %collective-permute-start) | collective-permute-done | bytes 786464 | tf_op jit(solution)/shard_map/ppermute | solution.py:242
  51.8 0.0 collective-permute-done.3.above_ref
  51.8 0.5 collective-permute-done.5.other_hbm
  52.3 9.6 %shard_map.39 = f32[8,3,8,2048]{3,2,1,0:T(8,128)} custom-call(s32[4]{0:T(128)S(1)} %pad_add_fusion.place_ref, f32[3,4,8,2048]{3,2,1,0:T(8,128)S(1)} %collective-permute-done.below_ref, f32[3,4,8,2048]{3,2,1,0:T(8,128)S(1)} %get-tuple-element.18.low_ref, f32[3,4,8,2048]{3,2,1,0:T(8,128)S(1)} %get-tuple-element.19.high_ref, ...), custom_call_target="tpu_custom_call" | custom-call | tf_op jit(solution)/shard_map/pallas_call | solution.py:268
  (2 shorter events, 0.0 us)
Async XLA Ops:
  0.8 9.5 %collective-permute-start.1 = (f32[3,8,128]{2,1,0:T(8,128)S(1)}, f32[3,8,128]{2,1,0:T(8,128)S(1)}, u32[]{:S(2)}, u32[]{:S(2)}) collective-permute-start(f32[3,8,128]{2,1,0:T(8,128)S(1)} %get-tuple-element.15), channel_id=1, source_target_pairs={{0,1},{1,2},{2,3},{3,4},{4,5},{5,6},{6,7},{7,8},{8,9},{9,10},{10,1... | collective-permute-start | bytes 36872 | tf_op jit(solution)/shard_map/ppermute | solution.py:258
  4.1 6.3 %collective-permute-start.2 = (f32[3,8,128]{2,1,0:T(8,128)S(1)}, f32[3,8,128]{2,1,0:T(8,128)S(1)}, u32[]{:S(2)}, u32[]{:S(2)}) collective-permute-start(f32[3,8,128]{2,1,0:T(8,128)S(1)} %get-tuple-element.16), channel_id=1, source_target_pairs={{1,0},{2,1},{3,2},{4,3},{5,4},{6,5},{7,6},{8,7},{9,8},{10,9},{11,1... | collective-permute-start | bytes 36872 | tf_op jit(solution)/shard_map/ppermute | solution.py:258
  8.3 1.4 %copy-start = (f32[8,3,8,2048]{3,2,1,0:T(8,128)S(1)}, f32[8,3,8,2048]{3,2,1,0:T(8,128)}, u32[]{:S(2)}) copy-start(f32[8,3,8,2048]{3,2,1,0:T(8,128)} %state_ref.1) | copy-start | bytes 4718596
  10.4 22.0 %collective-permute-start.4 = (f32[22,8,128]{2,1,0:T(8,128)S(1)}, f32[22,8,128]{2,1,0:T(8,128)S(1)}, u32[]{:S(2)}, u32[]{:S(2)}) collective-permute-start(f32[22,8,128]{2,1,0:T(8,128)S(1)} %pad_maximum_fusion.1), channel_id=1, source_target_pairs={{0,64},{64,0},{1,65},{65,1},{2,66},{66,2},{3,67},{67,3},{4,68},{68... | collective-permute-start | bytes 270344 | tf_op jit(solution)/shard_map/ppermute | solution.py:261
  24.9 26.9 %collective-permute-start = (f32[3,4,8,2048]{3,2,1,0:T(8,128)S(1)}, f32[3,4,8,2048]{3,2,1,0:T(8,128)S(1)}, u32[]{:S(2)}, u32[]{:S(2)}) collective-permute-start(f32[3,4,8,2048]{3,2,1,0:T(8,128)S(1)} %get-tuple-element.19.high_ref), channel_id=1, source_target_pairs={{0,1},{1,2},{2,3},{3,4},{4,5},{5,6},{6,7},{7,8},{8,9},{9,10},{10,1... | collective-permute-start | bytes 2359304 | tf_op jit(solution)/shard_map/ppermute | solution.py:242
  26.8 24.9 %collective-permute-start.3 = (f32[3,4,8,2048]{3,2,1,0:T(8,128)S(1)}, f32[3,4,8,2048]{3,2,1,0:T(8,128)}, u32[]{:S(2)}, u32[]{:S(2)}) collective-permute-start(f32[3,4,8,2048]{3,2,1,0:T(8,128)S(1)} %get-tuple-element.18.low_ref), channel_id=1, source_target_pairs={{1,0},{2,1},{3,2},{4,3},{5,4},{6,5},{7,6},{8,7},{9,8},{10,9},{11,1... | collective-permute-start | bytes 2359304 | tf_op jit(solution)/shard_map/ppermute | solution.py:243
  44.5 7.8 %collective-permute-start.5 = (f32[4,2,22,8,128]{4,3,2,1,0:T(8,128)S(1)}, f32[4,2,22,8,128]{4,3,2,1,0:T(8,128)}, u32[]{:S(2)}, u32[]{:S(2)}) collective-permute-start(f32[4,2,22,8,128]{4,3,2,1,0:T(8,128)S(1)} %bitcast.6), channel_id=1, source_target_pairs={{0,32},{32,0},{1,33},{33,1},{2,34},{34,2},{3,35},{35,3},{4,36},{36... | collective-permute-start | bytes 2162696 | tf_op jit(solution)/shard_map/ppermute | solution.py:263

commit v6 on v5

--- a/solution.py
+++ b/solution.py
@@ -27,11 +27,18 @@
     return pltpu.CompilerParams(vmem_limit_bytes=mebibytes << 20)
 
 
-def split_rows(state_ref, low_ref, high_ref):
+def split_rows(state_hbm, low_ref, high_ref, state_ref, sems):
     fields, rows, lon = state_ref.shape[1:]
     half = rows // 2
+    copies = [
+        pltpu.make_async_copy(state_hbm.at[:, field], state_ref.at[:, field], sems.at[field])
+        for field in range(fields)
+    ]
+    for copy in copies:
+        copy.start()
 
     for field in range(fields):
+        copies[field].wait()
 
         @pl.loop(0, lon // LANES)
         def _(tile):
@@ -49,10 +56,11 @@
     return pl.pallas_call(
         split_rows,
         out_shape=(half, half),
-        in_specs=[VMEM],
+        in_specs=[pl.BlockSpec(memory_space=pltpu.HBM)],
         out_specs=(VMEM, VMEM),
-        compiler_params=room(8),
-    )(state)
+        scratch_shapes=[pltpu.VMEM(state.shape, state.dtype), pltpu.SemaphoreType.DMA((fields,))],
+        compiler_params=room(4),
+    )(pltpu.with_memory_space_constraint(state, pltpu.HBM))
 
 
 def pack(wind_hbm, depth_hbm, own_ref, up_ref, down_ref, wind_ref, depth_ref, sems):

time: 62.2 us -> 62.1 us (level)
  the two profiles are of different devices: /device:TPU:33 before, /device:TPU:38 now
where the time goes in v6:
time: 62.1 us; the launch traced here: 61.8 us
  starting transfers between devices  32.6 us (52%)
  blocking collectives  13.6 us (22%)
  Pallas kernels  12.2 us (20%)
  waiting for transfers between devices  3.09 us (5%)
    ppermute x1, starting transfers between devices, shards(): mine = jnp.stack([own, lax.ppermute(own, 'zh', swap)])  14.8 us
    all_gather x1, blocking collectives, shards(): mine = lax.all_gather(mine, 'x', axis=0)  13.6 us
    pallas_call x1, Pallas kernels, shards(): pl.pallas_call(advance_all, out_shape=jax.ShapeDtypeStruct(perturbation.s...  9.62 us
    ppermute x1, starting transfers between devices, shards(): above = lax.ppermute(low, 'lat', down)  5.12 us
    ppermute x1, starting transfers between devices, shards(): lax.ppermute(to_down, 'lat', down)  4.47 us
    ppermute x1, starting transfers between devices, shards(): lax.ppermute(to_up, 'lat', up)  3.48 us
    ppermute x1, waiting for transfers between devices, shards(): below = lax.ppermute(high, 'lat', up)  3.08 us
    ppermute x1, starting transfers between devices, shards(): below = lax.ppermute(high, 'lat', up)  2.83 us
  transfers between devices with their start and end apart: 6, of which 1 were waited for; matrix products, arithmetic and copies ran while one was open for 0% of the time, Pallas kernels for 3%

profile of v6, /device:TPU:38, one launch (start us, length us, event | category | flops | bytes accessed | tf_op | source)
XLA Modules:
  0.0 61.8 jit_solution(11986244851046815146)
XLA Ops:
  0.0 0.8 %shard_map.38 = (f32[16,8,128]{2,1,0:T(8,128)S(1)}, f32[3,8,128]{2,1,0:T(8,128)S(1)}, f32[3,8,128]{2,1,0:T(8,128)S(1)}) custom-call(f32[4,3,8,128]{3,2,1,0:T(8,128)} %wind_hbm.1, f32[4,8,128]{2,1,0:T(8,128)} %depth_hbm.1), custom_call_target="tpu_custom_call" | custom-call | tf_op jit(solution)/shard_map/pallas_call | solution.py:254
  0.8 3.5 %collective-permute-start.1 = (f32[3,8,128]{2,1,0:T(8,128)S(1)}, f32[3,8,128]{2,1,0:T(8,128)S(1)}, u32[]{:S(2)}, u32[]{:S(2)}) collective-permute-start(f32[3,8,128]{2,1,0:T(8,128)S(1)} %get-tuple-element.15), channel_id=1, source_target_pairs={{0,1},{1,2},{2,3},{3,4},{4,5},{5,6},{6,7},{7,8},{8,9},{9,10},{10,1... | collective-permute-start | bytes 36872 | tf_op jit(solution)/shard_map/ppermute | solution.py:266
  4.3 4.5 %collective-permute-start.2 = (f32[3,8,128]{2,1,0:T(8,128)S(1)}, f32[3,8,128]{2,1,0:T(8,128)S(1)}, u32[]{:S(2)}, u32[]{:S(2)}) collective-permute-start(f32[3,8,128]{2,1,0:T(8,128)S(1)} %get-tuple-element.16), channel_id=1, source_target_pairs={{1,0},{2,1},{3,2},{4,3},{5,4},{6,5},{7,6},{8,7},{9,8},{10,9},{11,1... | collective-permute-start | bytes 36872 | tf_op jit(solution)/shard_map/ppermute | solution.py:266
  8.8 1.7 %shard_map.37 = (f32[3,4,8,2048]{3,2,1,0:T(8,128)S(1)}, f32[3,4,8,2048]{3,2,1,0:T(8,128)S(1)}) custom-call(f32[8,3,8,2048]{3,2,1,0:T(8,128)} %state_hbm.1), custom_call_target="tpu_custom_call" | custom-call | tf_op jit(solution)/shard_map/pallas_call | solution.py:56
  10.5 0.0 collective-permute-done.1
  10.6 0.0 collective-permute-done.2
  10.6 14.8 %collective-permute-start.4 = (f32[22,8,128]{2,1,0:T(8,128)S(1)}, f32[22,8,128]{2,1,0:T(8,128)S(1)}, u32[]{:S(2)}, u32[]{:S(2)}) collective-permute-start(f32[22,8,128]{2,1,0:T(8,128)S(1)} %pad_maximum_fusion.1), channel_id=1, source_target_pairs={{0,64},{64,0},{1,65},{65,1},{2,66},{66,2},{3,67},{67,3},{4,68},{68... | collective-permute-start | bytes 270344 | tf_op jit(solution)/shard_map/ppermute | solution.py:269
  25.4 2.8 %collective-permute-start = (f32[3,4,8,2048]{3,2,1,0:T(8,128)S(1)}, f32[3,4,8,2048]{3,2,1,0:T(8,128)S(1)}, u32[]{:S(2)}, u32[]{:S(2)}) collective-permute-start(f32[3,4,8,2048]{3,2,1,0:T(8,128)S(1)} %get-tuple-element.19.high_ref), channel_id=1, source_target_pairs={{0,1},{1,2},{2,3},{3,4},{4,5},{5,6},{6,7},{7,8},{8,9},{9,10},{10,1... | collective-permute-start | bytes 2359304 | tf_op jit(solution)/shard_map/ppermute | solution.py:250
  28.3 5.1 %collective-permute-start.3 = (f32[3,4,8,2048]{3,2,1,0:T(8,128)S(1)}, f32[3,4,8,2048]{3,2,1,0:T(8,128)}, u32[]{:S(2)}, u32[]{:S(2)}) collective-permute-start(f32[3,4,8,2048]{3,2,1,0:T(8,128)S(1)} %get-tuple-element.18.low_ref), channel_id=1, source_target_pairs={{1,0},{2,1},{3,2},{4,3},{5,4},{6,5},{7,6},{8,7},{9,8},{10,9},{11,1... | collective-permute-start | bytes 2359304 | tf_op jit(solution)/shard_map/ppermute | solution.py:251
  33.4 0.0 collective-permute-done.4
  33.4 13.6 %all-gather = f32[8,22,8,128]{3,2,1,0:T(8,128)S(1)} all-gather(f32[2,22,8,128]{3,2,1,0:T(8,128)S(1)} %pad_maximum_fusion), channel_id=2, replica_groups=mesh['x'=4,'zh'=2,'core'=2,'lat'=32] {'x'}, dimensions={0}, use_global_device_ids=true | all-gather | bytes 901120 | tf_op jit(solution)/shard_map/all_gather | solution.py:270
  47.1 1.9 %collective-permute-start.5 = (f32[4,2,22,8,128]{4,3,2,1,0:T(8,128)S(1)}, f32[4,2,22,8,128]{4,3,2,1,0:T(8,128)}, u32[]{:S(2)}, u32[]{:S(2)}) collective-permute-start(f32[4,2,22,8,128]{4,3,2,1,0:T(8,128)S(1)} %bitcast.6), channel_id=1, source_target_pairs={{0,32},{32,0},{1,33},{33,1},{2,34},{34,2},{3,35},{35,3},{4,36},{36... | collective-permute-start | bytes 2162696 | tf_op jit(solution)/shard_map/ppermute | solution.py:271
  49.0 0.1 pad_add_fusion.place_ref
  49.1 3.1 %collective-permute-done.below_ref = f32[3,4,8,2048]{3,2,1,0:T(8,128)S(1)} collective-permute-done((f32[3,4,8,2048]{3,2,1,0:T(8,128)S(1)}, f32[3,4,8,2048]{3,2,1,0:T(8,128)S(1)}, u32[]{:S(2)}, u32[]{:S(2)}) %collective-permute-start) | collective-permute-done | bytes 786464 | tf_op jit(solution)/shard_map/ppermute | solution.py:250
  52.1 0.0 collective-permute-done.3.above_ref
  52.1 0.0 collective-permute-done.5.other_hbm
  52.1 9.6 %shard_map.39 = f32[8,3,8,2048]{3,2,1,0:T(8,128)} custom-call(s32[4]{0:T(128)S(1)} %pad_add_fusion.place_ref, f32[3,4,8,2048]{3,2,1,0:T(8,128)S(1)} %collective-permute-done.below_ref, f32[3,4,8,2048]{3,2,1,0:T(8,128)S(1)} %get-tuple-element.18.low_ref, f32[3,4,8,2048]{3,2,1,0:T(8,128)S(1)} %get-tuple-element.19.high_ref, ...), custom_call_target="tpu_custom_call" | custom-call | tf_op jit(solution)/shard_map/pallas_call | solution.py:276
  (2 shorter events, 0.0 us)
Async XLA Ops:
  0.8 9.7 %collective-permute-start.1 = (f32[3,8,128]{2,1,0:T(8,128)S(1)}, f32[3,8,128]{2,1,0:T(8,128)S(1)}, u32[]{:S(2)}, u32[]{:S(2)}) collective-permute-start(f32[3,8,128]{2,1,0:T(8,128)S(1)} %get-tuple-element.15), channel_id=1, source_target_pairs={{0,1},{1,2},{2,3},{3,4},{4,5},{5,6},{6,7},{7,8},{8,9},{9,10},{10,1... | collective-permute-start | bytes 36872 | tf_op jit(solution)/shard_map/ppermute | solution.py:266
  4.3 6.2 %collective-permute-start.2 = (f32[3,8,128]{2,1,0:T(8,128)S(1)}, f32[3,8,128]{2,1,0:T(8,128)S(1)}, u32[]{:S(2)}, u32[]{:S(2)}) collective-permute-start(f32[3,8,128]{2,1,0:T(8,128)S(1)} %get-tuple-element.16), channel_id=1, source_target_pairs={{1,0},{2,1},{3,2},{4,3},{5,4},{6,5},{7,6},{8,7},{9,8},{10,9},{11,1... | collective-permute-start | bytes 36872 | tf_op jit(solution)/shard_map/ppermute | solution.py:266
  10.6 22.8 %collective-permute-start.4 = (f32[22,8,128]{2,1,0:T(8,128)S(1)}, f32[22,8,128]{2,1,0:T(8,128)S(1)}, u32[]{:S(2)}, u32[]{:S(2)}) collective-permute-start(f32[22,8,128]{2,1,0:T(8,128)S(1)} %pad_maximum_fusion.1), channel_id=1, source_target_pairs={{0,64},{64,0},{1,65},{65,1},{2,66},{66,2},{3,67},{67,3},{4,68},{68... | collective-permute-start | bytes 270344 | tf_op jit(solution)/shard_map/ppermute | solution.py:269
  25.4 26.7 %collective-permute-start = (f32[3,4,8,2048]{3,2,1,0:T(8,128)S(1)}, f32[3,4,8,2048]{3,2,1,0:T(8,128)S(1)}, u32[]{:S(2)}, u32[]{:S(2)}) collective-permute-start(f32[3,4,8,2048]{3,2,1,0:T(8,128)S(1)} %get-tuple-element.19.high_ref), channel_id=1, source_target_pairs={{0,1},{1,2},{2,3},{3,4},{4,5},{5,6},{6,7},{7,8},{8,9},{9,10},{10,1... | collective-permute-start | bytes 2359304 | tf_op jit(solution)/shard_map/ppermute | solution.py:250
  28.3 23.9 %collective-permute-start.3 = (f32[3,4,8,2048]{3,2,1,0:T(8,128)S(1)}, f32[3,4,8,2048]{3,2,1,0:T(8,128)}, u32[]{:S(2)}, u32[]{:S(2)}) collective-permute-start(f32[3,4,8,2048]{3,2,1,0:T(8,128)S(1)} %get-tuple-element.18.low_ref), channel_id=1, source_target_pairs={{1,0},{2,1},{3,2},{4,3},{5,4},{6,5},{7,6},{8,7},{9,8},{10,9},{11,1... | collective-permute-start | bytes 2359304 | tf_op jit(solution)/shard_map/ppermute | solution.py:251
  47.1 5.1 %collective-permute-start.5 = (f32[4,2,22,8,128]{4,3,2,1,0:T(8,128)S(1)}, f32[4,2,22,8,128]{4,3,2,1,0:T(8,128)}, u32[]{:S(2)}, u32[]{:S(2)}) collective-permute-start(f32[4,2,22,8,128]{4,3,2,1,0:T(8,128)S(1)} %bitcast.6), channel_id=1, source_target_pairs={{0,32},{32,0},{1,33},{33,1},{2,34},{34,2},{3,35},{35,3},{4,36},{36... | collective-permute-start | bytes 2162696 | tf_op jit(solution)/shard_map/ppermute | solution.py:271
